TPU v7x, 128 devices: a whole 4x4x4 slice. The times are simulated.
128 devices in a mesh: tracer: 8 (over y, x_lo), domain: 16 (over x_hi, z, core).
Axes of the slice: x: 4 (x_hi: 2, x_lo: 2; x = x_hi * 2 + x_lo), y: 4, z: 4, core: 2. Of those that a mesh axis runs over, the one named last changes fastest.
Arguments:
- log_rate: float32 [256, 256, 256], P('domain'), may hold values from -1.6 to 0
- velocity: float32 [256, 256], replicated, may hold values from 0.2 to 1
- initial: float32 [8, 256, 256, 256], P('tracer', 'domain'), may hold values from -6 to 6
- profile: float32 [8, 256, 256], P('tracer'), may hold values from 0.5 to 4
- plane: int32 [8], P('tracer'), may hold values from 0 to 255
- depth: int32 [8, 32768], P('tracer'), may hold values from 0 to 255
- row: int32 [8, 32768], P('tracer'), may hold values from 0 to 255
- column: int32 [8, 32768], P('tracer'), may hold values from 0 to 255
- step_of: int32 [8, 32768], P('tracer'), may hold values from 1 to 2
- observed: float32 [8, 32768], P('tracer'), may hold values from -6 to 6
Outputs:
- smoothed_gradient: float32 [128, 128, 128], P('domain', 'tracer')
All inputs are finite; a program needn't handle non-finite values.
Results may differ from a plain program's by a relative error of at most 0.0003.
Values sent between devices are 32-bit elements; how exact they have to be, the bound alone decides.
No kernel may reach another device: no remote copies, remote signals or barrier semaphores. Data moves between devices by JAX's collectives and lax.ppermute only.
A program may use at most 512 MiB of HBM per device.

v0:
```python
import math

import jax
import jax.numpy as jnp
from jax import lax
from jax.sharding import PartitionSpec as P

R = 2
STEPS = 2


TIME_STEP = 0.14
PRIOR_RANGE = 4.0


def extended(array, sides, width):
    for axis, dim in sides:
        count, length = (lax.axis_size(axis), array.shape[dim])
        up = [(i, (i + 1) % count) for i in range(count)]
        down = [(j, i) for i, j in up]
        last = lax.slice_in_dim(array, length - width, length, axis=dim)
        initial = lax.slice_in_dim(array, 0, width, axis=dim)
        before = lax.ppermute(last, axis, up)
        after = lax.ppermute(initial, axis, down)
        array = jnp.concatenate([before, array, after], axis=dim)
    return array


def diffusion(padded, faces):
    values = padded[1:-1]
    result = faces[0] * (padded[2:] - values) - faces[1] * (values - padded[:-2])
    for axis_dim, face_now, face_back in ((1, faces[2], faces[3]), (2, faces[4], faces[5])):
        ahead_cell = jnp.roll(values, -1, axis_dim)
        behind_cell = jnp.roll(values, 1, axis_dim)
        result = result + face_now * (ahead_cell - values) - face_back * (values - behind_cell)
    return result


def sensitivity(state_pad, adjoint_pad):
    state = state_pad[1:-1]
    adjoint = adjoint_pad[1:-1]
    upper_term = (state_pad[2:] - state) * (adjoint_pad[2:] - adjoint)
    lower_term = (state - state_pad[:-2]) * (adjoint - adjoint_pad[:-2])
    result = upper_term + lower_term
    for axis_dim in (1, 2):
        product = (jnp.roll(state, -1, axis_dim) - state) * (
            jnp.roll(adjoint, -1, axis_dim) - adjoint
        )
        result = result + product + jnp.roll(product, 1, axis_dim)
    return -0.5 * result


def hartley(length, first_row, count):
    indices = first_row + lax.iota(jnp.int32, count)
    phases = indices[:, None] * lax.iota(jnp.int32, length)[None, :] % length
    angles = 2.0 * math.pi / length * phases.astype(jnp.float32)
    return jnp.cos(angles) + jnp.sin(angles)


def transform(table, values, axis_dim):
    forms = ("kj,jab->kab", "kj,ajb->akb", "kj,abj->abk")
    return jnp.einsum(
        forms[axis_dim],
        table,
        values,
        precision=lax.Precision.HIGHEST,
        preferred_element_type=jnp.float32,
    )


def symbol_part(length, first_row, count):
    indices = (first_row + lax.iota(jnp.int32, count)) % length
    angles = 2.0 * math.pi / length * indices.astype(jnp.float32)
    return 2.0 - 2.0 * jnp.cos(angles)


def prior_weights(
    depth_span,
    depth_first,
    depth_count,
    first_span,
    first_start,
    first_count,
    second_span,
    second_start,
    second_count,
):
    lam_sum = (
        symbol_part(depth_span, depth_first, depth_count)[:, None, None]
        + symbol_part(first_span, first_start, first_count)[None, :, None]
        + symbol_part(second_span, second_start, second_count)[None, None, :]
    )
    factor = 1.0 + PRIOR_RANGE * lam_sum
    return 1.0 / (factor * factor) / (depth_span * first_span * second_span)


def local(log_rate, velocity, initial, profile, plane, depth, row, column, step_of, observed):
    slab_depth, rows_count, cols_count = log_rate.shape
    offset = lax.axis_index("domain") * slab_depth
    kappa_field = jnp.exp(log_rate)
    kappa_pad = extended(kappa_field, (("domain", 0),), 1)
    face_first = 0.5 * (kappa_field + jnp.roll(kappa_field, -1, 1))
    face_second = 0.5 * (kappa_field + jnp.roll(kappa_field, -1, 2))
    faces = (
        0.5 * (kappa_pad[1:-1] + kappa_pad[2:]),
        0.5 * (kappa_pad[:-2] + kappa_pad[1:-1]),
        face_first,
        jnp.roll(face_first, 1, 1),
        face_second,
        jnp.roll(face_second, 1, 2),
    )
    layers = offset + lax.iota(jnp.int32, slab_depth)
    source = jnp.where((layers == plane[0])[:, None, None], profile[0][None], 0.0)
    wind = velocity[None]
    local_depth = depth[0] - offset
    inside = (local_depth >= 0) & (local_depth < slab_depth)
    flat = (
        jnp.clip(local_depth, 0, slab_depth - 1) * (rows_count * cols_count)
        + row[0] * cols_count
        + column[0]
    )
    probe_steps = step_of[0]
    states = []
    values = initial[0]
    sampled = jnp.zeros_like(observed[0])
    for section in range(STEPS):
        padded = extended(values, (("domain", 0),), 1)
        states.append(padded)
        values = (
            padded[1:-1]
            + TIME_STEP * (diffusion(padded, faces) - wind * (padded[1:-1] - padded[:-2]))
            + TIME_STEP * source
        )
        sampled = jnp.where(probe_steps == section + 1, values.reshape(-1)[flat], sampled)
    residual = jnp.where(inside, sampled - observed[0], 0.0)

    def inject(section):
        empty = jnp.zeros((slab_depth * rows_count * cols_count,), log_rate.dtype)
        return (
            empty.at[flat]
            .add(jnp.where(probe_steps == section, residual, 0.0))
            .reshape(log_rate.shape)
        )

    adjoint = inject(STEPS)
    gradient = jnp.zeros_like(log_rate)
    for section in reversed(range(STEPS)):
        adjoint_pad = extended(adjoint, (("domain", 0),), 1)
        gradient = gradient + sensitivity(states[section], adjoint_pad)
        if section > 0:
            adjoint = (
                adjoint_pad[1:-1]
                + TIME_STEP
                * (diffusion(adjoint_pad, faces) - wind * (adjoint_pad[1:-1] - adjoint_pad[2:]))
                + inject(section)
            )
    fine_grad = TIME_STEP * kappa_field * gradient
    coarse = fine_grad.reshape(slab_depth // R, R, rows_count // R, R, cols_count // R, R).sum(
        axis=(1, 3, 5)
    )
    coarse_depth, first_size, second_size = coarse.shape
    domain_count = lax.axis_size("domain")
    tracer_count = lax.axis_size("tracer")
    share_rows = first_size // tracer_count
    own_first = lax.axis_index("tracer") * share_rows
    summed = lax.psum(coarse, "tracer")
    spectral = transform(hartley(first_size, 0, first_size), summed, 1)
    spectral = transform(hartley(second_size, 0, second_size), spectral, 2)
    columns = lax.all_to_all(spectral, "domain", split_axis=1, concat_axis=0, tiled=True)
    full_depth = columns.shape[0]
    block_width = first_size // domain_count
    depth_table = hartley(full_depth, 0, full_depth)
    columns = transform(depth_table, columns, 0)
    columns = columns * prior_weights(
        full_depth,
        0,
        full_depth,
        first_size,
        lax.axis_index("domain") * block_width,
        block_width,
        second_size,
        0,
        second_size,
    )
    columns = transform(depth_table, columns, 0)
    returned = lax.all_to_all(columns, "domain", split_axis=0, concat_axis=1, tiled=True)
    returned = transform(hartley(second_size, 0, second_size), returned, 2)
    result = transform(hartley(first_size, own_first, share_rows), returned, 1)
    return result


def solution(mesh):
    return jax.shard_map(
        local,
        mesh=mesh,
        in_specs=(
            P("domain", None, None),
            P(),
            P("tracer", "domain", None, None),
            P("tracer", None, None),
            P("tracer"),
            P("tracer", None),
            P("tracer", None),
            P("tracer", None),
            P("tracer", None),
            P("tracer", None),
        ),
        out_specs=P("domain", "tracer", None),
        check_vma=False,
    )
```

profile of v0, /device:TPU:1, one launch (start us, length us, event | category | flops | bytes accessed | tf_op | source)
XLA Modules:
  0.0 1856.5 jit_solution(17200851356653741827)
XLA Ops:
  14.3 4.4 collective-permute-start.1
  24.6 4.7 fusion.144
  39.8 5.7 fusion.28
  46.1 4.4 copy-done.4
  51.2 17.0 fusion.36
  68.3 4.8 fusion.139
  73.1 4.2 fusion.141
  78.1 5.4 collective-permute-start.4
  86.4 4.2 copy.37
  90.6 387.0 %gather_fusion.1 = f32[32768]{0:T(1024)S(1)} fusion(f32[1048576]{0:T(1024)} %bitcast.57, s32[32768]{0:T(1024)S(1)} %copy-done.16), kind=kCustom, calls=%fused_computation.1 | custom fusion | bytes 393216 | tf_op jit(solution)/shard_map/gather | solution.py:134
  478.6 22.2 %fusion.46 = f32[16,256,256]{2,1,0:T(8,128)S(1)} fusion(f32[16,256,256]{2,1,0:T(8,128)} %copy-done, f32[16,255,256]{2,1,0:T(8,128)} %get-tuple-element.30, f32[16,1,256]{2,1,0:T(1,128)S(1)} %get-tuple-element.32, f32[16,256,255]{2,1,0:T(8,128)} %get-tuple-element.26, f32[16,256,1]{2,1,0:T(8,128)} %get-tuple-element.28, f32[16,256,256]{2,1,0:T(8,128)} %copy-done.6, ...), kind=kLoop, calls=%fused_computation.70 | loop fusion | flops 39845888 | bytes 47710224 | tf_op jit(solution)/shard_map/add | solution.py:130
  500.8 4.2 copy.36
  505.1 386.5 %gather_fusion = f32[32768]{0:T(1024)S(1)} fusion(f32[1048576]{0:T(1024)} %bitcast.56, s32[32768]{0:T(1024)S(1)} %copy-done.16), kind=kCustom, calls=%fused_computation | custom fusion | bytes 393216 | tf_op jit(solution)/shard_map/gather | solution.py:134
  891.7 173.9 %scatter_custom_fusion = f32[1048576]{0:T(1024)} fusion(s32[32768]{0:T(1024)} %bitcast.81, f32[32768]{0:T(1024)S(1)} %get-tuple-element.7, f32[]{:T(128)} %constant.93.clone.1), kind=kCustom, calls=%fused_computation.93 | custom fusion | flops 32768 | bytes 4194816 | tf_op jit(solution)/shard_map/scatter-add | solution.py:141
  1065.6 5.3 reshape.196
  1070.8 8.2 fusion.134
  1079.0 4.0 fusion.136
  1087.7 8.1 collective-permute-start.6
  1096.6 10.8 fusion.61
  1112.0 173.3 %scatter_custom_fusion.1 = f32[1048576]{0:T(1024)} fusion(s32[32768]{0:T(1024)} %bitcast.82, f32[32768]{0:T(1024)} %broadcast_select_fusion.1, f32[]{:T(128)} %constant.93.clone.1), kind=kCustom, calls=%fused_computation.91 | custom fusion | flops 32768 | bytes 4194816 | tf_op jit(solution)/shard_map/scatter-add | solution.py:141
  1285.4 5.2 reshape.197
  1290.6 23.6 %fusion.19 = f32[16,256,256]{2,1,0:T(8,128)S(1)} fusion(f32[16,256,256]{2,1,0:T(8,128)} %reshape.197, f32[16,256,256]{2,1,0:T(8,128)} %reshape.196, f32[1,256,256]{2,1,0:T(8,128)S(1)} %collective-permute-done.6, f32[16,255,256]{2,1,0:T(8,128)} %get-tuple-element.20, f32[16,1,256]{2,1,0:T(1,128)S(1)} %get-tuple-element.22, ...), kind=kLoop, calls=%fused_computation.27 | loop fusion | flops 38797312 | bytes 51642368 | tf_op jit(solution)/shard_map/add | solution.py:152
  1323.3 5.4 collective-permute-start.8
  1328.7 8.3 fusion.55
  1342.1 29.1 %fusion.9 = f32[16,256,256]{2,1,0:T(8,128)} fusion(f32[16,256,256]{2,1,0:T(8,128)} %copy-done.11, f32[16,256,256]{2,1,0:T(8,128)} %get-tuple-element.11, f32[16,256,256]{2,1,0:T(8,128)} %copy-done.9, f32[1,256,256]{2,1,0:T(8,128)} %collective-permute-done.9, f32[1,256,256]{2,1,0:T(8,128)} %collective-permute-done.8, f32[16,256,256]{2,1,0:T(8,128)} %copy-done.10, ...), kind=kLoop, calls=%fused_computation.14 | loop fusion | flops 39845888 | bytes 60817408 | tf_op jit(solution)/shard_map/mul | solution.py:157
  1371.1 270.4 %reshape.198 = f32[8,2,128,2,128,2]{5,4,3,2,1,0:T(8,128)} reshape(f32[16,256,256]{2,1,0:T(8,128)} %fusion.9) | data formatting | bytes 8388608 | tf_op jit(solution)/shard_map/reshape | solution.py:158
  1641.5 80.2 %reduce_sum.9 = f32[8,128,128]{2,1,0:T(8,128)S(1)} reduce(f32[8,2,128,2,128,2]{5,4,3,2,1,0:T(8,128)} %reshape.198, f32[]{:T(128)} %constant.93.clone.1), dimensions={1,3,5}, to_apply=%region_2.3 | reduce | flops 917504 | bytes 4718596 | tf_op jit(solution)/shard_map/reduce_sum | solution.py:158
  1722.7 79.0 %all-reduce.2.cloned.1.call-done = f32[8,128,128]{1,2,0:T(8,128)} async-done(((f32[8,128,128]{1,2,0:T(8,128)}), f32[8,128,128]{1,2,0:T(8,128)}) %all-reduce.2.cloned.1.call-update) | async-done | bytes 524304 | tf_op jit(solution)/shard_map/psum | solution.py:166
  1805.5 11.8 all-to-all-start
  1817.5 11.1 all-to-all-done
  1831.6 4.5 all-to-all-start.1
  1836.2 11.4 all-to-all-done.1
  (135 shorter events, 63.4 us)
Async XLA Ops:
  6.5 1795.2 %all-reduce.2.cloned.1.call-start = ((), (), s32[]{:S(2)}) async-start(), calls=%async_computation.2 | async-start | bytes 1048576 | tf_op jit(solution)/shard_map/psum | solution.py:166
  9.5 15.0 copy-start.8
  10.4 40.8 %collective-permute-start = (f32[1,256,256]{2,1,0:T(8,128)}, f32[1,256,256]{2,1,0:T(8,128)S(1)}, u32[]{:S(2)}, u32[]{:S(2)}) collective-permute-start(f32[1,256,256]{2,1,0:T(8,128)} %get-tuple-element.44), channel_id=1, source_target_pairs={{1,0},{2,1},{3,2},{4,3},{5,4},{6,5},{7,6},{8,7},{9,8},{10,9},{11,1... | collective-permute-start | bytes 786440 | tf_op jit(solution)/shard_map/ppermute | solution.py:24
  11.8 39.4 %collective-permute-start.2 = (f32[1,256,256]{2,1,0:T(8,128)}, f32[1,256,256]{2,1,0:T(8,128)}, u32[]{:S(2)}, u32[]{:S(2)}) collective-permute-start(f32[1,256,256]{2,1,0:T(8,128)} %get-tuple-element.43), channel_id=1, source_target_pairs={{0,1},{1,2},{2,3},{3,4},{4,5},{5,6},{6,7},{7,8},{8,9},{9,10},{10,1... | collective-permute-start | bytes 786440 | tf_op jit(solution)/shard_map/ppermute | solution.py:23
  14.3 36.9 %collective-permute-start.1 = (f32[1,256,256]{2,1,0:T(8,128)}, f32[1,256,256]{2,1,0:T(8,128)}, u32[]{:S(2)}, u32[]{:S(2)}) collective-permute-start(f32[1,256,256]{2,1,0:T(8,128)} %get-tuple-element.45), channel_id=1, source_target_pairs={{1,0},{2,1},{3,2},{4,3},{5,4},{6,5},{7,6},{8,7},{9,8},{10,9},{11,1... | collective-permute-start | bytes 786440 | tf_op jit(solution)/shard_map/ppermute | solution.py:24
  18.7 32.5 %collective-permute-start.3 = (f32[1,256,256]{2,1,0:T(8,128)}, f32[1,256,256]{2,1,0:T(8,128)}, u32[]{:S(2)}, u32[]{:S(2)}) collective-permute-start(f32[1,256,256]{2,1,0:T(8,128)} %get-tuple-element.46), channel_id=1, source_target_pairs={{0,1},{1,2},{2,3},{3,4},{4,5},{5,6},{6,7},{7,8},{8,9},{9,10},{10,1... | collective-permute-start | bytes 786440 | tf_op jit(solution)/shard_map/ppermute | solution.py:23
  39.8 11.5 copy-start.15
  45.4 22.8 %copy-start.6 = (f32[16,256,256]{2,1,0:T(8,128)}, f32[16,256,256]{2,1,0:T(8,128)S(1)}, u32[]{:S(2)}) copy-start(f32[16,256,256]{2,1,0:T(8,128)S(1)} %get-tuple-element.48) | copy-start | bytes 12582916
  45.5 22.8 %copy-start.7 = (f32[16,256,256]{2,1,0:T(8,128)}, f32[16,256,256]{2,1,0:T(8,128)S(1)}, u32[]{:S(2)}) copy-start(f32[16,256,256]{2,1,0:T(8,128)S(1)} %get-tuple-element.47) | copy-start | bytes 12582916
  68.3 18.1 copy-start
  78.1 400.4 %collective-permute-start.4 = (f32[1,256,256]{2,1,0:T(8,128)}, f32[1,256,256]{2,1,0:T(8,128)S(1)}, u32[]{:S(2)}, u32[]{:S(2)}) collective-permute-start(f32[1,256,256]{2,1,0:T(8,128)} %get-tuple-element.33), channel_id=1, source_target_pairs={{1,0},{2,1},{3,2},{4,3},{5,4},{6,5},{7,6},{8,7},{9,8},{10,9},{11,1... | collective-permute-start | bytes 786440 | tf_op jit(solution)/shard_map/ppermute | solution.py:24
  83.5 395.1 %collective-permute-start.5 = (f32[1,256,256]{2,1,0:T(8,128)}, f32[1,256,256]{2,1,0:T(8,128)}, u32[]{:S(2)}, u32[]{:S(2)}) collective-permute-start(f32[1,256,256]{2,1,0:T(8,128)} %get-tuple-element.34), channel_id=1, source_target_pairs={{0,1},{1,2},{2,3},{3,4},{4,5},{5,6},{6,7},{7,8},{8,9},{9,10},{10,1... | collective-permute-start | bytes 786440 | tf_op jit(solution)/shard_map/ppermute | solution.py:23
  90.6 388.0 %copy-start.17 = (f32[1,256,256]{2,1,0:T(8,128)S(1)}, f32[1,256,256]{2,1,0:T(8,128)}, u32[]{:S(2)}) copy-start(f32[1,256,256]{2,1,0:T(8,128)} %param.13) | copy-start | bytes 786436
  478.5 22.3 %copy-start.18 = (f32[1,256,256]{2,1,0:T(8,128)}, f32[1,256,256]{2,1,0:T(8,128)S(1)}, u32[]{:S(2)}) copy-start(f32[1,256,256]{2,1,0:T(8,128)S(1)} %collective-permute-done.4) | copy-start | bytes 786436
  505.1 386.5 %copy-start.25 = (pred[32768]{0:T(1024)(128)(4,1)S(1)}, pred[32768]{0:T(1024)(128)(4,1)}, u32[]{:S(2)}) copy-start(pred[32768]{0:T(1024)(128)(4,1)} %get-tuple-element.6) | copy-start | bytes 98308
  505.1 386.5 %copy-start.30 = (f32[1,32768]{1,0:T(1,128)S(1)}, f32[1,32768]{1,0:T(1,128)}, u32[]{:S(2)}) copy-start(f32[1,32768]{1,0:T(1,128)} %param.19) | copy-start | bytes 393220
  505.1 386.5 %copy-start.31 = (pred[32768]{0:T(1024)(128)(4,1)S(1)}, pred[32768]{0:T(1024)(128)(4,1)}, u32[]{:S(2)}) copy-start(pred[32768]{0:T(1024)(128)(4,1)} %get-tuple-element.5) | copy-start | bytes 98308
  505.1 386.5 %copy-start.32 = (pred[32768]{0:T(1024)(128)(4,1)S(1)}, pred[32768]{0:T(1024)(128)(4,1)}, u32[]{:S(2)}) copy-start(pred[32768]{0:T(1024)(128)(4,1)} %get-tuple-element.49) | copy-start | bytes 98308
  1087.7 202.9 %collective-permute-start.6 = (f32[1,256,256]{2,1,0:T(8,128)S(1)}, f32[1,256,256]{2,1,0:T(8,128)S(1)}, u32[]{:S(2)}, u32[]{:S(2)}) collective-permute-start(f32[1,256,256]{2,1,0:T(8,128)S(1)} %slice.298), channel_id=1, source_target_pairs={{1,0},{2,1},{3,2},{4,3},{5,4},{6,5},{7,6},{8,7},{9,8},{10,9},{11,1... | collective-permute-start | bytes 786440 | tf_op jit(solution)/shard_map/ppermute | solution.py:24
  1096.6 194.0 %collective-permute-start.7 = (f32[1,256,256]{2,1,0:T(8,128)}, f32[1,256,256]{2,1,0:T(8,128)S(1)}, u32[]{:S(2)}, u32[]{:S(2)}) collective-permute-start(f32[1,256,256]{2,1,0:T(8,128)} %slice.301), channel_id=1, source_target_pairs={{0,1},{1,2},{2,3},{3,4},{4,5},{5,6},{6,7},{7,8},{8,9},{9,10},{10,1... | collective-permute-start | bytes 786440 | tf_op jit(solution)/shard_map/ppermute | solution.py:23
  1290.6 23.6 %copy-start.20 = (f32[1,256,256]{2,1,0:T(8,128)}, f32[1,256,256]{2,1,0:T(8,128)S(1)}, u32[]{:S(2)}) copy-start(f32[1,256,256]{2,1,0:T(8,128)S(1)} %collective-permute-done.6) | copy-start | bytes 786436
  1290.6 23.6 %copy-start.22 = (f32[1,256,256]{2,1,0:T(8,128)}, f32[1,256,256]{2,1,0:T(8,128)S(1)}, u32[]{:S(2)}) copy-start(f32[1,256,256]{2,1,0:T(8,128)S(1)} %collective-permute-done.7) | copy-start | bytes 786436
  1314.2 14.4 copy-start.9
  1317.0 11.6 copy-start.13
  1317.0 11.6 copy-start.14
  1320.3 8.4 copy-start.26
  1323.3 18.7 %collective-permute-start.8 = (f32[1,256,256]{2,1,0:T(8,128)}, f32[1,256,256]{2,1,0:T(8,128)}, u32[]{:S(2)}, u32[]{:S(2)}) collective-permute-start(f32[1,256,256]{2,1,0:T(8,128)} %get-tuple-element.13), channel_id=1, source_target_pairs={{1,0},{2,1},{3,2},{4,3},{5,4},{6,5},{7,6},{8,7},{9,8},{10,9},{11,1... | collective-permute-start | bytes 786440 | tf_op jit(solution)/shard_map/ppermute | solution.py:24
  1328.7 13.4 collective-permute-start.9
  1328.7 13.3 copy-start.19
  1328.7 13.3 copy-start.21
  1805.5 23.1 %all-to-all-start = ((f32[8,128,128]{2,0,1:T(8,128)}), f32[8,128,128]{2,0,1:T(8,128)S(1)}, u32[]{:S(2)}, u32[]{:S(2)}) async-start(f32[8,128,128]{2,0,1:T(8,128)} %fusion.73), calls=%async_computation | async-start | bytes 1048576 | tf_op jit(solution)/shard_map/all_to_all | solution.py:169
  1831.6 15.9 all-to-all-start.1
  (16 other events, 73.0 us)
Sparse Core Ops, SparseCore 0:
  1722.9 78.8 all-reduce.1
where the time goes:
time: 1890 us; the launch traced here: 1860 us
  local copies, waits for them, and re-layouts  1140 us (60%)
  other arithmetic  548 us (29%)
  waiting for transfers between devices  102 us (5%)
  starting transfers between devices  43 us (2%)
    gather x2, local copies, waits for them, and re-layouts, local(): values.reshape(-1)[flat]  773 us
    scatter-add x2, other arithmetic, inject(): return empty.at[flat].add(jnp.where(probe_steps == section, residual, 0.0...  347 us
    reshape x1, local copies, waits for them, and re-layouts, local(): fine_grad.reshape(slab_depth // R, R, rows_count // R, R, cols_count // R...  270 us
    reduce_sum x1, other arithmetic, local(): fine_grad.reshape(slab_depth // R, R, rows_count // R, R, cols_count // R...  80.2 us
    psum x1, waiting for transfers between devices, local(): summed = lax.psum(coarse, 'tracer')  79 us
    add x2, other arithmetic, local(): padded[1:-1]  39.3 us
  transfers between devices with their start and end apart: 13, of which 3 were waited for; matrix products, arithmetic and copies ran while one was open for 34% of the time, Pallas kernels for 0%

commit v1 on v0

v1 whole, which is shorter than its diff:
```python
import functools
import math

import jax
import jax.numpy as jnp
import numpy as np
from jax import lax
from jax.experimental import pallas as pl
from jax.experimental.pallas import tpu as pltpu
from jax.sharding import PartitionSpec as P

R = 2
STEPS = 2
TIME_STEP = 0.14
PRIOR_RANGE = 4.0

HALO = 4
LEAD = 2
LANES = 128
LONG, SHORT = 8, 4
PAD = 8
STRIP = 32


def hartley(length):
    phases = np.outer(np.arange(length), np.arange(length)) % length
    angles = 2.0 * math.pi / length * phases
    return (np.cos(angles) + np.sin(angles)).astype(np.float32)


def symbol(length):
    return (2.0 - 2.0 * np.cos(2.0 * math.pi / length * np.arange(length))).astype(np.float32)


def sort_kernel(
    offset_ref,
    depth_ref,
    row_ref,
    column_ref,
    step_ref,
    observed_ref,
    keys_out,
    values_out,
    starts_out,
    keys,
    values,
):
    offset = offset_ref[0]
    plane = (depth_ref[...] - (offset - LEAD)) & 255
    key = (plane << 17) | ((step_ref[...] - 1) << 16) | (row_ref[...] << 8) | column_ref[...]
    keys[...] = key.reshape(keys.shape)
    values[...] = observed_ref[...].reshape(values.shape)
    for index in range(starts_out.shape[0]):
        if index == 0:
            starts_out[index] = 0
        else:
            starts_out[index] = jnp.sum((key < (index << 17)).astype(jnp.int32))

    lane = lax.broadcasted_iota(jnp.int32, (8, LANES), 1)
    sublane = lax.broadcasted_iota(jnp.int32, (8, LANES), 0)

    def pair(low, high, down):
        (key_a, value_a), (key_b, value_b) = low, high
        if down is False:
            swap = key_a > key_b
        elif down is True:
            swap = key_a < key_b
        else:
            swap = jnp.logical_xor(key_a > key_b, down)
        return (
            (jnp.where(swap, key_b, key_a), jnp.where(swap, value_b, value_a)),
            (jnp.where(swap, key_a, key_b), jnp.where(swap, value_a, value_b)),
        )

    def within(item, axis, distance, upper, largest):
        key, value = item
        size = key.shape[axis]
        key_p = jnp.where(
            upper, pltpu.roll(key, distance, axis), pltpu.roll(key, size - distance, axis)
        )
        value_p = jnp.where(
            upper, pltpu.roll(value, distance, axis), pltpu.roll(value, size - distance, axis)
        )
        gap = key_p - key
        take = jnp.where(largest, gap, -gap) > 0
        return jnp.where(take, key_p, key), jnp.where(take, value_p, value)

    def bit_of(array, bit):
        return ((array >> bit) & 1) == 1

    def registers(items, level, down):
        for bit in range(level, -1, -1):
            for low in range(16):
                if low & (1 << bit):
                    continue
                high = low | (1 << bit)
                order = down(low) if callable(down) else down
                items[low], items[high] = pair(items[low], items[high], order)
        return items

    def sublanes(items, bit, down):
        upper = bit_of(sublane, bit)
        largest = jnp.logical_xor(upper, down) if not isinstance(down, bool) else (
            jnp.logical_not(upper) if down else upper
        )
        return [within(item, 0, 1 << bit, upper, largest) for item in items]

    def load(group):
        return [(keys[group * 16 + i], values[group * 16 + i]) for i in range(16)]

    def store(group, items):
        for i, (key, value) in enumerate(items):
            keys[group * 16 + i] = key
            values[group * 16 + i] = value

    for group in range(2):
        items = load(group)
        for level in range(1, 4):
            items = registers(
                items, level - 1, lambda low, level=level: bool((low >> level) & 1)
            )
        items = registers(items, 3, bit_of(sublane, 0))
        for level in range(1, 3):
            down = bit_of(sublane, level)
            for bit in range(level - 1, -1, -1):
                items = sublanes(items, bit, down)
            items = registers(items, 3, down)
        down = bool(group)
        for bit in range(2, -1, -1):
            items = sublanes(items, bit, down)
        items = registers(items, 3, down)
        store(group, items)

    def merge(level, carry):
        down = ((lane >> level) & 1) == 1

        def across(turn, inner):
            bit = level - 1 - turn
            distance = jnp.int32(1) << bit
            upper = ((lane >> bit) & 1) == 1
            largest = jnp.logical_xor(upper, down)
            for i in range(32):
                keys[i], values[i] = within((keys[i], values[i]), 1, distance, upper, largest)
            return inner

        lax.fori_loop(0, level, across, 0)
        for i in range(16):
            low, high = pair((keys[i], values[i]), (keys[i + 16], values[i + 16]), down)
            keys[i], values[i] = low
            keys[i + 16], values[i + 16] = high
        for group in range(2):
            items = load(group)
            for bit in range(2, -1, -1):
                items = sublanes(items, bit, down)
            items = registers(items, 3, down)
            store(group, items)
        return carry

    lax.fori_loop(0, 8, merge, 0)

    for half in range(2):
        part = keys[pl.ds(half * 16, 16)].reshape(LANES, LANES)
        keys_out[pl.ds(half, LANES, 2), :] = part.T
        part = values[pl.ds(half * 16, 16)].reshape(LANES, LANES)
        values_out[pl.ds(half, LANES, 2), :] = part.T
    keys_out[2 * LANES :, :] = jnp.full((8, LANES), -1, jnp.int32)
    values_out[2 * LANES :, :] = jnp.zeros((8, LANES), jnp.float32)


def sort_probes(offset, depth, row, column, step_of, observed, planes):
    count = depth.size
    shape = (count // LANES, LANES)
    vmem = pl.BlockSpec(memory_space=pltpu.VMEM)
    smem = pl.BlockSpec(memory_space=pltpu.SMEM)
    return pl.pallas_call(
        sort_kernel,
        out_shape=(
            jax.ShapeDtypeStruct((shape[0] + 8, LANES), jnp.int32),
            jax.ShapeDtypeStruct((shape[0] + 8, LANES), jnp.float32),
            jax.ShapeDtypeStruct((planes + 1,), jnp.int32),
        ),
        in_specs=[smem] + [vmem] * 5,
        out_specs=(vmem, vmem, smem),
        scratch_shapes=[
            pltpu.VMEM((shape[0] // 8, 8, LANES), jnp.int32),
            pltpu.VMEM((shape[0] // 8, 8, LANES), jnp.float32),
        ],
        compiler_params=pltpu.CompilerParams(vmem_limit_bytes=16 * 2**20),
        cost_estimate=pl.CostEstimate(flops=20_000_000, bytes_accessed=2**20, transcendentals=0),
        name="sort_probes",
    )(offset, *(a.reshape(shape) for a in (depth, row, column, step_of, observed)))


def bin_kernel(starts, keys_ref, values_ref, *fields):
    place = pl.program_id(0)
    size = fields[0].shape[1]
    both = STEPS * size
    counts, sums = fields[:STEPS], fields[STEPS:]
    begin, end = starts[place], starts[place + 1]
    first = begin >> 7
    windows = (end - (first << 7) + 2 * LANES - 1) >> 8

    def window(turn):
        at = first + 2 * turn
        key = jnp.concatenate([keys_ref[pl.ds(at, 1), :], keys_ref[pl.ds(at + 1, 1), :]], axis=1)
        value = jnp.concatenate(
            [values_ref[pl.ds(at, 1), :], values_ref[pl.ds(at + 1, 1), :]], axis=1
        )
        target = lax.broadcasted_iota(jnp.int32, (both, 2 * LANES), 0) + (place << 9)
        in_row = jnp.where((key >> 8) == target, 1.0, 0.0).astype(jnp.bfloat16)
        in_column = (key & 255) == lax.broadcasted_iota(jnp.int32, (size, 2 * LANES), 0)
        coarse = value.astype(jnp.bfloat16).astype(jnp.float32)
        rest = value - coarse

        def product(amount):
            return lax.dot_general(
                in_row,
                jnp.where(in_column, amount, 0.0).astype(jnp.bfloat16),
                (((1,), (1,)), ((), ())),
                preferred_element_type=jnp.float32,
            )

        return product(1.0), product(coarse) + product(rest)

    def parts(pair):
        for fields_of, values in zip((counts, sums), pair):
            for step, field in enumerate(fields_of):
                yield field, values[step * size : (step + 1) * size]

    for field, value in parts(window(0)):
        field[0] = value

    def more(turn, carry):
        for field, value in parts(window(turn)):
            field[0] += value
        return carry

    lax.fori_loop(1, windows, more, 0)


def bin_probes(starts, keys, values, rows_count, cols_count):
    places = starts.shape[0] - 1
    vmem = pl.BlockSpec(memory_space=pltpu.VMEM)
    block = pl.BlockSpec((1, rows_count, cols_count), lambda i: (i, 0, 0))
    field = jax.ShapeDtypeStruct((places, rows_count, cols_count), jnp.float32)
    return pl.pallas_call(
        bin_kernel,
        grid=(places,),
        out_shape=(field,) * (2 * STEPS),
        in_specs=[pl.BlockSpec(memory_space=pltpu.SMEM), vmem, vmem],
        out_specs=(block,) * (2 * STEPS),
        compiler_params=pltpu.CompilerParams(
            vmem_limit_bytes=8 * 2**20, dimension_semantics=("arbitrary",)
        ),
        cost_estimate=pl.CostEstimate(
            flops=30_000_000, bytes_accessed=20 * 2**20, transcendentals=0
        ),
        name="bin_probes",
    )(starts, keys, values)


def ahead(parts):
    lane = lax.broadcasted_iota(jnp.int32, parts[0].shape, 1)
    left, right = (pltpu.roll(part, LANES - 1, 1) for part in parts)
    last = lane == LANES - 1
    return jnp.where(last, right, left), jnp.where(last, left, right)


def behind(parts):
    lane = lax.broadcasted_iota(jnp.int32, parts[0].shape, 1)
    left, right = (pltpu.roll(part, 1, 1) for part in parts)
    first = lane == 0
    return jnp.where(first, right, left), jnp.where(first, left, right)


def sweep_kernel(
    source_plane,
    rate_low,
    rate_own,
    rate_high,
    state_low,
    state_own,
    state_high,
    velocity_ref,
    profile_ref,
    count1,
    count2,
    sum1,
    sum2,
    columns_table,
    out_ref,
    half_rate,
    state0,
    state1,
    adjoint2,
    adjoint1,
    face_x,
    grad_x0,
    grad_x1,
    grad_x2,
    inject1,
    depth_product,
    pair_sum,
    coarse_rows,
):
    index = pl.program_id(0)
    total = pl.num_programs(0)
    size = half_rate.shape[2] - 2 * PAD
    halves = range(2)
    strips = range(0, size, STRIP)

    def rows(ref, plane, half, start, shift=0):
        slot = plane & (ref.shape[0] - 1)
        return ref[slot, half, PAD + start + shift : PAD + start + shift + STRIP, :]

    def put(ref, plane, half, start, value):
        slot = plane & (ref.shape[0] - 1)
        ref[slot, half, PAD + start : PAD + start + STRIP, :] = value
        if start == 0:
            ref[slot, half, PAD + size : PAD + size + 1, :] = value[:1]
        if start + STRIP == size:
            ref[slot, half, PAD - 1 : PAD, :] = value[STRIP - 1 :]

    def plain(ref, plane, half, start):
        return ref[plane & (ref.shape[0] - 1), half, start : start + STRIP, :]

    def put_plain(ref, plane, half, start, value):
        ref[plane & (ref.shape[0] - 1), half, start : start + STRIP, :] = value

    def enter(rate_ref, state_ref):
        for start in strips:
            span = slice(start, start + STRIP)
            rate, state = [], []
            for half in halves:
                cols = slice(half * LANES, (half + 1) * LANES)
                rate.append((0.5 * TIME_STEP) * jnp.exp(rate_ref[0, span, cols]))
                state.append(state_ref[0, span, cols])
            rate_ahead, state_ahead = ahead(rate), ahead(state)
            for half in halves:
                put(half_rate, index, half, start, rate[half])
                put(state0, index, half, start, state[half])
                put_plain(face_x, index, half, start, rate[half] + rate_ahead[half])
                put_plain(grad_x0, index, half, start, state_ahead[half] - state[half])

    @pl.when(index < HALO)
    def _():
        enter(rate_low, state_low)

    @pl.when((index >= HALO) & (index < total - HALO))
    def _():
        enter(rate_own, state_own)

    @pl.when((index >= total - HALO) & (index < total))
    def _():
        enter(rate_high, state_high)

    def advance(field, grad_x, slot, start, adjoint):
        up, down = slot + 1, slot - 1
        flux = [
            plain(face_x, slot, half, start) * plain(grad_x, slot, half, start) for half in halves
        ]
        flux_behind = behind(flux)
        result = []
        for half in halves:
            value = rows(field, slot, half, start)
            rate = rows(half_rate, slot, half, start)
            wind = TIME_STEP * velocity_ref[
                start : start + STRIP, half * LANES : (half + 1) * LANES
            ]
            rate_up = rate + rows(half_rate, up, half, start)
            rate_down = rate + rows(half_rate, down, half, start)
            if adjoint:
                rate_up = rate_up + wind
            else:
                rate_down = rate_down + wind
            depth_part = rate_up * (rows(field, up, half, start) - value) - rate_down * (
                value - rows(field, down, half, start)
            )
            row_part = (rate + rows(half_rate, slot, half, start, 1)) * (
                rows(field, slot, half, start, 1) - value
            ) - (rate + rows(half_rate, slot, half, start, -1)) * (
                value - rows(field, slot, half, start, -1)
            )
            result.append(value + depth_part + row_part + (flux[half] - flux_behind[half]))
        return result

    def save(field, grad_x, slot, start, parts):
        parts_ahead = ahead(parts)
        for half in halves:
            put(field, slot, half, start, parts[half])
            put_plain(grad_x, slot, half, start, parts_ahead[half] - parts[half])

    def source_gain(plane):
        return jnp.where(plane == source_plane[0], jnp.float32(TIME_STEP), jnp.float32(0.0))

    def source(gain, half, start):
        return gain * profile_ref[0, start : start + STRIP, half * LANES : (half + 1) * LANES]

    plane1 = index - 1

    @pl.when((plane1 >= 1) & (plane1 < total - 1))
    def _():
        slot = plane1
        gain = source_gain(plane1)
        for start in strips:
            parts = advance(state0, grad_x0, slot, start, False)
            parts = [parts[half] + source(gain, half, start) for half in halves]
            save(state1, grad_x1, slot, start, parts)

    plane2 = index - 2

    @pl.when((plane2 >= 2) & (plane2 < total - 2))
    def _():
        slot = plane2
        gain = source_gain(plane2)
        for start in strips:
            parts = advance(state1, grad_x1, slot, start, False)
            mu = []
            for half in halves:
                cols = slice(half * LANES, (half + 1) * LANES)
                state2 = parts[half] + source(gain, half, start)
                span = slice(start, start + STRIP)
                mu.append(count2[0, span, cols] * state2 - sum2[0, span, cols])
                put_plain(
                    inject1,
                    slot,
                    half,
                    start,
                    count1[0, span, cols] * rows(state1, slot, half, start) - sum1[0, span, cols],
                )
            save(adjoint2, grad_x2, slot, start, mu)

    plane3 = index - 3

    @pl.when((plane3 >= 3) & (plane3 < total - 3))
    def _():
        slot = plane3
        for start in strips:
            parts = advance(adjoint2, grad_x2, slot, start, True)
            for half in halves:
                put(
                    adjoint1,
                    slot,
                    half,
                    start,
                    parts[half] + plain(inject1, slot, half, start),
                )

    plane4 = index - 4

    def products(slot, other, half, start):
        def step(field):
            return rows(field, other, half, start) - rows(field, slot, half, start)

        return step(state0) * step(adjoint1) + step(state1) * step(adjoint2)

    @pl.when(plane4 == HALO - 1)
    def _():
        slot = plane4
        for start in strips:
            for half in halves:
                depth_product[half, start : start + STRIP, :] = products(
                    slot, slot + 1, half, start
                )

    @pl.when(plane4 >= HALO)
    def _():
        slot, up = plane4, plane4 + 1
        even = (plane4 & 1) == 0
        for start in strips:
            mu = [rows(adjoint1, slot, half, start) for half in halves]
            mu_ahead = ahead(mu)
            product_x = [
                plain(grad_x0, slot, half, start) * (mu_ahead[half] - mu[half])
                + plain(grad_x1, slot, half, start) * plain(grad_x2, slot, half, start)
                for half in halves
            ]
            product_behind = behind(product_x)
            for half in halves:
                span = slice(start, start + STRIP)
                result = product_x[half] + product_behind[half]
                upper = products(slot, up, half, start)
                result = result + (upper + depth_product[half, span, :])
                depth_product[half, span, :] = upper
                for shift in (1, -1):
                    factors = [
                        rows(field, slot, half, start, shift) - rows(field, slot, half, start)
                        for field in (state0, adjoint1, state1, adjoint2)
                    ]
                    result = result + (factors[0] * factors[1] + factors[2] * factors[3])
                result = -rows(half_rate, slot, half, start) * result
                pair_sum[half, span, :] = jnp.where(even, 0.0, pair_sum[half, span, :]) + result

    @pl.when((plane4 >= HALO) & ((plane4 & 1) == 1))
    def _():
        for half in halves:
            even_rows = pair_sum[half, pl.ds(0, size // R, R), :]
            odd_rows = pair_sum[half, pl.ds(1, size // R, R), :]
            cols = slice(half * LANES, (half + 1) * LANES)
            coarse_rows[(plane4 - HALO) >> 1, :, cols] = even_rows + odd_rows

    @pl.when(index == total - 1)
    def _():
        planes = coarse_rows.shape[0]
        for plane in range(planes):
            out_ref[pl.ds(plane, columns_table.shape[0], planes), :] = lax.dot_general(
                columns_table[...],
                coarse_rows[plane],
                (((1,), (1,)), ((), ())),
                precision=lax.Precision.HIGHEST,
                preferred_element_type=jnp.float32,
            )


def sweep(source_plane, rates, states, velocity, profile, fields):
    own, rows_count, cols_count = rates[1].shape
    total = own + 2 * HALO
    coarse = rows_count // R
    plane = (1, rows_count, cols_count)
    smem = pl.BlockSpec(memory_space=pltpu.SMEM)
    vmem = pl.BlockSpec(memory_space=pltpu.VMEM)
    low = pl.BlockSpec(plane, lambda i: (jnp.minimum(i, HALO - 1), 0, 0))
    middle = pl.BlockSpec(plane, lambda i: (jnp.clip(i - HALO, 0, own - 1), 0, 0))
    high = pl.BlockSpec(plane, lambda i: (jnp.clip(i - HALO - own, 0, HALO - 1), 0, 0))
    columns_table = jnp.asarray(np.repeat(hartley(cols_count // R), R, axis=1))
    voxels = pl.BlockSpec(
        (1, rows_count, cols_count),
        lambda i: (jnp.clip(i - HALO, 0, total - 2 * LEAD - 1), 0, 0),
    )
    def padded(kept):
        return pltpu.VMEM((kept, 2, rows_count + 2 * PAD, LANES), jnp.float32)

    def plain(kept):
        return pltpu.VMEM((kept, 2, rows_count, LANES), jnp.float32)

    return pl.pallas_call(
        sweep_kernel,
        grid=(total,),
        out_shape=jax.ShapeDtypeStruct((cols_count // R * (own // R), coarse), jnp.float32),
        in_specs=[smem, low, middle, high, low, middle, high, vmem, vmem] + [voxels] * 4 + [vmem],
        out_specs=vmem,
        scratch_shapes=[padded(LONG)] * 2
        + [padded(SHORT)] * 3
        + [plain(SHORT), plain(LONG), plain(SHORT), plain(SHORT), plain(2)]
        + [
            pltpu.VMEM((2, rows_count, LANES), jnp.float32),
            pltpu.VMEM((2, rows_count, LANES), jnp.float32),
            pltpu.VMEM((own // R, coarse, cols_count), jnp.float32),
        ],
        compiler_params=pltpu.CompilerParams(
            vmem_limit_bytes=19 * 2**20, dimension_semantics=("arbitrary",)
        ),
        cost_estimate=pl.CostEstimate(
            flops=200_000_000, bytes_accessed=34 * 2**20, transcendentals=0
        ),
        name="sweep",
    )(
        source_plane,
        *rates,
        *states,
        velocity,
        profile,
        *fields,
        columns_table,
    )


def exact_dot(a, b):
    return jnp.dot(a, b, precision=lax.Precision.HIGHEST, preferred_element_type=jnp.float32)


def filter_kernel(lam_second, received, table_ref, symbol_depth, symbol_rows, out_ref, field):
    depth_blocks, tracers, planes, size = received.shape
    for block in range(depth_blocks):
        field[block * planes : (block + 1) * planes, :] = jnp.sum(received[block], axis=0)
    table = table_ref[...]
    spectrum = exact_dot(exact_dot(table, field[...]), table)
    lam = symbol_depth[...] + symbol_rows[...] + lam_second[0]
    factor = 1.0 + PRIOR_RANGE * lam
    spectrum = spectrum * (1.0 / (factor * factor) / float(size**3))
    field[...] = exact_dot(exact_dot(table, spectrum), table)
    share = size // tracers
    group = lax.broadcasted_iota(jnp.int32, (depth_blocks, size), 1) // share
    by_plane = [field[pl.ds(plane, depth_blocks, planes), :] for plane in range(planes)]
    for tracer in range(tracers):
        part = jnp.zeros((depth_blocks, size), jnp.float32)
        for plane in range(planes):
            shift = (plane - tracer) * share % size
            moved = pltpu.roll(by_plane[plane], shift, 1) if shift else by_plane[plane]
            part = jnp.where(group == plane, moved, part)
        out_ref[pl.ds(tracer, depth_blocks, tracers), :] = part


def filtered(received, own_symbol):
    depth_blocks, tracers, planes, size = received.shape
    line = symbol(size)
    vmem = pl.BlockSpec(memory_space=pltpu.VMEM)
    return pl.pallas_call(
        filter_kernel,
        out_shape=jax.ShapeDtypeStruct((depth_blocks * tracers, size), jnp.float32),
        in_specs=[pl.BlockSpec(memory_space=pltpu.SMEM)] + [vmem] * 4,
        out_specs=vmem,
        scratch_shapes=[pltpu.VMEM((depth_blocks * planes, size), jnp.float32)],
        compiler_params=pltpu.CompilerParams(vmem_limit_bytes=16 * 2**20),
        name="filter",
    )(
        own_symbol,
        received,
        jnp.asarray(hartley(size)),
        jnp.asarray(line[:, None]),
        jnp.asarray(line[None, :]),
    )


def inverse_kernel(received, table_ref, out_ref):
    out_ref[...] = lax.dot_general(
        received[...],
        table_ref[...],
        (((0,), (0,)), ((), ())),
        precision=lax.Precision.HIGHEST,
        preferred_element_type=jnp.float32,
    )


def inverse_columns(received):
    vmem = pl.BlockSpec(memory_space=pltpu.VMEM)
    return pl.pallas_call(
        inverse_kernel,
        out_shape=jax.ShapeDtypeStruct(received.shape, jnp.float32),
        in_specs=[vmem, vmem],
        out_specs=vmem,
        compiler_params=pltpu.CompilerParams(vmem_limit_bytes=16 * 2**20),
        name="inverse_columns",
    )(received, jnp.asarray(hartley(received.shape[0])))


def neighbours(array):
    count = lax.axis_size("domain")
    up = [(i, (i + 1) % count) for i in range(count)]
    down = [(j, i) for i, j in up]
    before = lax.ppermute(array[-HALO:], "domain", up)
    after = lax.ppermute(array[:HALO], "domain", down)
    return before, array, after


def local(log_rate, velocity, initial, profile, plane, depth, row, column, step_of, observed):
    slab, rows_count, cols_count = log_rate.shape
    domain_count, tracer_count = lax.axis_size("domain"), lax.axis_size("tracer")
    full = slab * domain_count
    offset = lax.axis_index("domain") * slab
    rates = neighbours(log_rate)
    states = neighbours(initial[0])
    keys, values, starts = sort_probes(
        offset.astype(jnp.int32)[None],
        depth,
        row,
        column,
        step_of,
        observed,
        slab + 2 * LEAD,
    )
    source_plane = (plane - (offset - HALO)) % full
    fields = bin_probes(starts, keys, values, rows_count, cols_count)
    spectral = sweep(source_plane, rates, states, velocity, profile, fields)
    first, planes, second = rows_count // R, slab // R, cols_count // R
    axes = ("domain", "tracer")
    received = lax.all_to_all(
        spectral.reshape(second, planes, first), axes, split_axis=0, concat_axis=0, tiled=True
    )
    own = lax.axis_index("domain") * tracer_count + lax.axis_index("tracer")
    own_symbol = lax.dynamic_slice(jnp.asarray(symbol(second)), (own,), (1,))
    back = filtered(received.reshape(domain_count, tracer_count, planes, first), own_symbol)
    result = lax.all_to_all(back, axes, split_axis=0, concat_axis=0, tiled=True)
    return inverse_columns(result).reshape(planes, first // tracer_count, second)


def solution(mesh):
    return jax.shard_map(
        local,
        mesh=mesh,
        in_specs=(
            P("domain", None, None),
            P(),
            P("tracer", "domain", None, None),
            P("tracer", None, None),
            P("tracer"),
            P("tracer", None),
            P("tracer", None),
            P("tracer", None),
            P("tracer", None),
            P("tracer", None),
        ),
        out_specs=P("domain", "tracer", None),
        check_vma=False,
    )
```

time: 1890 us -> 118 us (0.06); the launches traced: 1860 us -> 118 us
  local copies, waits for them, and re-layouts: 1140 us -> 9.72 us
  other arithmetic: 548 us -> 0 us
  waiting for transfers between devices: 102 us -> 12.6 us
  Pallas kernels: 0 us -> 60 us
  starting transfers between devices: 43 us -> 21.2 us
    gather x2 -> x0, local copies, waits for them, and re-layouts: 773 us -> none  [local(): values.reshape(-1)[flat]]
    scatter-add x2 -> x0, other arithmetic: 347 us -> none  [inject(): return empty.at[flat].add(jnp.where(probe_steps == section, residual, 0.0...]
    reshape x3 -> x0, local copies, waits for them, and re-layouts: 281 us -> none  [the longest x1 270 us: local(): fine_grad.reshape(slab_depth // R, R, rows_count // R, R, cols_count // R...]
    reduce_sum x1 -> x0, other arithmetic: 80.2 us -> none  [local(): fine_grad.reshape(slab_depth // R, R, rows_count // R, R, cols_count // R...]
    psum x1 -> x0, waiting for transfers between devices: 79 us -> none  [local(): summed = lax.psum(coarse, 'tracer')]
    add x5 -> x0, other arithmetic: 62.9 us -> none  [the longest x2 39.3 us: local(): padded[1:-1]]
    slice x34 -> x2, local copies, waits for them, and re-layouts: 65.1 us -> 4.71 us  [neighbours(): after = lax.ppermute(array[:HALO], 'domain', down)]
    pallas_call x0 -> x5, Pallas kernels: none -> 60 us  [the longest x1 38.2 us: sweep(): pl.pallas_call(sweep_kernel, grid=(total,), out_shape=jax.ShapeDtypeStruc...]
  transfers between devices with their start and end apart: 13 -> 5, of which waited for: 3 -> 1; matrix products, arithmetic and copies ran while one was open for 34% -> 2% of each run, Pallas kernels for 0% -> 16%
where the time goes in v1:
time: 118 us
  Pallas kernels  60 us (51%)
  starting transfers between devices  21.2 us (18%)
  blocking collectives  13.9 us (12%)
  waiting for transfers between devices  12.6 us (11%)
  local copies, waits for them, and re-layouts  9.72 us (8%)
    pallas_call x1, Pallas kernels, sweep(): pl.pallas_call(sweep_kernel, grid=(total,), out_shape=jax.ShapeDtypeStruc...  38.2 us
    all_to_all x1, blocking collectives, local(): result = lax.all_to_all(back, axes, split_axis=0, concat_axis=0, tiled=True)  13.9 us
    all_to_all x1, starting transfers between devices, local(): lax.all_to_all(spectral.reshape(second, planes, first), axes, split_axis=...  13.8 us
    all_to_all x1, waiting for transfers between devices, local(): lax.all_to_all(spectral.reshape(second, planes, first), axes, split_axis=...  12.6 us
    pallas_call x1, Pallas kernels, bin_probes(): pl.pallas_call(bin_kernel, grid=(places,), out_shape=(field,) * (2 * STEP...  10.5 us
    pallas_call x1, Pallas kernels, sort_probes(): pl.pallas_call(sort_kernel, out_shape=(jax.ShapeDtypeStruct((shape[0] + 8...  8.74 us
    ppermute x2, starting transfers between devices, neighbours(): after = lax.ppermute(array[:HALO], 'domain', down)  5.82 us
    slice x2, local copies, waits for them, and re-layouts, neighbours(): after = lax.ppermute(array[:HALO], 'domain', down)  4.71 us
  transfers between devices with their start and end apart: 5, of which 1 were waited for; matrix products, arithmetic and copies ran while one was open for 2% of the time, Pallas kernels for 16%

profile of v1, /device:TPU:1, one launch (start us, length us, event | category | flops | bytes accessed | tf_op | source)
XLA Modules:
  0.0 118.3 jit_solution(13127389305515376746)
XLA Ops:
  0.0 0.0 copy-start.10
  0.0 0.0 copy-start.9
  0.0 0.0 copy-start.8
  0.0 0.0 copy-start.7
  0.0 0.0 copy-start.4
  0.1 0.0 copy-start.3
  0.1 3.2 %fusion = (f32[4,256,256]{2,1,0:T(8,128)}, f32[4,256,256]{2,1,0:T(8,128)}) fusion(f32[16,256,256]{2,1,0:T(8,128)} %rate_own.1), kind=kLoop, calls=%fused_computation.2 | loop fusion | bytes 4194304 | tf_op jit(solution)/shard_map/slice | solution.py:642
  3.3 1.4 %collective-permute-start.1 = (f32[4,256,256]{2,1,0:T(8,128)}, f32[4,256,256]{2,1,0:T(8,128)S(1)}, u32[]{:S(2)}, u32[]{:S(2)}) collective-permute-start(f32[4,256,256]{2,1,0:T(8,128)} %get-tuple-element.21), channel_id=1, source_target_pairs={{1,0},{2,1},{3,2},{4,3},{5,4},{6,5},{7,6},{8,7},{9,8},{10,9},{11,1... | collective-permute-start | bytes 3145736 | tf_op jit(solution)/shard_map/ppermute | solution.py:642
  4.7 1.6 %collective-permute-start = (f32[4,256,256]{2,1,0:T(8,128)}, f32[4,256,256]{2,1,0:T(8,128)}, u32[]{:S(2)}, u32[]{:S(2)}) collective-permute-start(f32[4,256,256]{2,1,0:T(8,128)} %get-tuple-element.22), channel_id=1, source_target_pairs={{0,1},{1,2},{2,3},{3,4},{4,5},{5,6},{6,7},{7,8},{8,9},{9,10},{10,1... | collective-permute-start | bytes 3145736 | tf_op jit(solution)/shard_map/ppermute | solution.py:641
  6.3 0.0 copy-done.1
  6.3 1.5 %slice_bitcast_fusion = (f32[4,256,256]{2,1,0:T(8,128)}, f32[4,256,256]{2,1,0:T(8,128)}) fusion(f32[1,16,256,256]{3,2,1,0:T(8,128)S(1)} %copy-done.1), kind=kLoop, calls=%fused_computation | loop fusion | bytes 4194304 | tf_op jit(solution)/shard_map/slice | solution.py:642
  7.8 4.4 %collective-permute-start.3 = (f32[4,256,256]{2,1,0:T(8,128)}, f32[4,256,256]{2,1,0:T(8,128)}, u32[]{:S(2)}, u32[]{:S(2)}) collective-permute-start(f32[4,256,256]{2,1,0:T(8,128)} %get-tuple-element.19), channel_id=1, source_target_pairs={{1,0},{2,1},{3,2},{4,3},{5,4},{6,5},{7,6},{8,7},{9,8},{10,9},{11,1... | collective-permute-start | bytes 3145736 | tf_op jit(solution)/shard_map/ppermute | solution.py:642
  12.2 0.0 collective-permute-start.2
  12.9 0.0 copy-done.11
  12.9 0.0 copy-done.10
  13.0 8.7 %sort_probes.1 = (s32[264,128]{1,0:T(8,128)S(1)}, f32[264,128]{1,0:T(8,128)S(1)}, s32[21]{0:T(128)S(1)}) custom-call(s32[1]{0:T(128)} %bitcast.4.offset_ref, s32[256,128]{1,0:T(8,128)S(1)} %bitcast.23, s32[256,128]{1,0:T(8,128)S(1)} %bitcast.24, s32[256,128]{1,0:T(8,128)S(1)} %bitcast.25, s32[256,128]{1,0:T(8,128)S(1)} %bitcast.26, f32[256,128]{1,0:T(8,128)S(1)} %bitcast.27), custom_call_target="tpu_custom_call" | custom-call | flops 20000000 | bytes 1048576 | tf_op jit(solution)/shard_map/sort_probes/pallas_call | solution.py:175
  21.7 10.5 %bin_probes.1 = (f32[20,256,256]{2,1,0:T(8,128)S(1)}, f32[20,256,256]{2,1,0:T(8,128)S(1)}, f32[20,256,256]{2,1,0:T(8,128)S(1)}, f32[20,256,256]{2,1,0:T(8,128)S(1)}) custom-call(s32[21]{0:T(128)S(1)} %get-tuple-element.12.starts, s32[264,128]{1,0:T(8,128)S(1)} %get-tuple-element.13.keys_ref, f32[264,128]{1,0:T(8,128)S(1)} %get-tuple-element.14.values_ref), custom_call_target="tpu_custom_call" | custom-call | flops 30000000 | bytes 20971520 | tf_op jit(solution)/shard_map/bin_probes/pallas_call | solution.py:246
  32.2 0.0 collective-permute-done.1.rate_high
  32.2 0.0 collective-permute-done.rate_low
  32.2 0.0 collective-permute-done.3.state_high
  32.2 0.0 collective-permute-done.2.state_low
  32.3 0.0 copy-start
  32.3 2.2 %copy-done = f32[16,256,256]{2,1,0:T(8,128)S(1)} copy-done((f32[16,256,256]{2,1,0:T(8,128)S(1)}, f32[16,256,256]{2,1,0:T(8,128)}, u32[]{:S(2)}) %copy-start) | copy-done | bytes 4194328
  34.5 2.2 %copy-done.2 = f32[1,16,256,256]{3,2,1,0:T(8,128)S(1)} copy-done((f32[1,16,256,256]{3,2,1,0:T(8,128)S(1)}, f32[1,16,256,256]{3,2,1,0:T(8,128)}, u32[]{:S(2)}) %copy-start.2) | copy-done | bytes 4194328
  36.7 38.2 %sweep.1 = f32[1024,128]{1,0:T(8,128)} custom-call(s32[1]{0:T(128)S(6)} %select_n.11.source_plane, f32[4,256,256]{2,1,0:T(8,128)} %collective-permute-done.rate_low, f32[16,256,256]{2,1,0:T(8,128)S(1)} %copy-done, f32[4,256,256]{2,1,0:T(8,128)S(1)} %collective-permute-done.1.rate_high, f32[4,256,256]{2,1,0:T(8,128)} %collective-permute-done.2.state_low, ...), custom_call_target="tpu_custom_call" | custom-call | flops 200000000 | bytes 35651584 | tf_op jit(solution)/shard_map/sweep/pallas_call | solution.py:536
  74.8 13.8 %all-to-all-start = ((f32[128,8,128]{2,1,0:T(8,128)}), f32[128,8,128]{2,1,0:T(8,128)S(1)}, u32[]{:S(2)}, u32[]{:S(2)}) async-start(f32[128,8,128]{2,1,0:T(8,128)} %bitcast.10), calls=%async_computation | async-start | bytes 1048576 | tf_op jit(solution)/shard_map/all_to_all | solution.py:667
  88.6 0.6 dynamic_slice.3.lam_second
  89.2 12.6 %all-to-all-done = f32[128,8,128]{2,1,0:T(8,128)S(1)} async-done(((f32[128,8,128]{2,1,0:T(8,128)}), f32[128,8,128]{2,1,0:T(8,128)S(1)}, u32[]{:S(2)}, u32[]{:S(2)}) %all-to-all-start) | async-done | bytes 524320 | tf_op jit(solution)/shard_map/all_to_all | solution.py:667
  101.8 0.0 copy-done.12
  101.8 1.7 %filter.1 = f32[128,128]{1,0:T(8,128)S(1)} custom-call(f32[1]{0:T(128)} %dynamic_slice.3.lam_second, f32[16,8,8,128]{3,2,1,0:T(8,128)S(1)} %bitcast.20, f32[128,128]{1,0:T(8,128)S(1)} %copy-done.5, f32[128,1]{1,0:T(8,128)S(1)} %copy-done.12, f32[1,128]{1,0:T(1,128)S(1)} %copy-done.13), custom_call_target="tpu_custom_call" | custom-call | tf_op jit(solution)/shard_map/filter/pallas_call | solution.py:598
  103.5 13.9 %all_to_all.16 = f32[128,1,128]{2,1,0:T(1,128)S(1)} all-to-all(f32[128,1,128]{2,1,0:T(1,128)S(1)} %bitcast.22), channel_id=1, replica_groups=mesh['tracer'=8,'domain'=16] {'domain','tracer'}, dimensions={0} | all-to-all | bytes 131072 | tf_op jit(solution)/shard_map/all_to_all | solution.py:673
  117.4 0.9 inverse_columns.1
  (17 shorter events, 0.0 us)
Async XLA Ops:
  0.0 6.3 %copy-start.1 = (f32[1,16,256,256]{3,2,1,0:T(8,128)S(1)}, f32[1,16,256,256]{3,2,1,0:T(8,128)}, u32[]{:S(2)}) copy-start(f32[1,16,256,256]{3,2,1,0:T(8,128)} %param.18) | copy-start | bytes 12582916
  0.0 32.2 %copy-start.6 = (f32[128,256]{1,0:T(8,128)S(1)}, f32[128,256]{1,0:T(8,128)}, u32[]{:S(2)}) copy-start(f32[128,256]{1,0:T(8,128)} %constant.49.clone.columns_table) | copy-start | bytes 393220
  0.0 12.9 %copy-start.11 = (f32[1,32768]{1,0:T(1,128)S(1)}, f32[1,32768]{1,0:T(1,128)}, u32[]{:S(2)}) copy-start(f32[1,32768]{1,0:T(1,128)} %param.25) | copy-start | bytes 393220
  0.0 12.9 %copy-start.10 = (s32[1,32768]{1,0:T(1,128)S(1)}, s32[1,32768]{1,0:T(1,128)}, u32[]{:S(2)}) copy-start(s32[1,32768]{1,0:T(1,128)} %param.24) | copy-start | bytes 393220
  0.0 12.9 %copy-start.9 = (s32[1,32768]{1,0:T(1,128)S(1)}, s32[1,32768]{1,0:T(1,128)}, u32[]{:S(2)}) copy-start(s32[1,32768]{1,0:T(1,128)} %param.23) | copy-start | bytes 393220
  0.0 12.9 %copy-start.8 = (s32[1,32768]{1,0:T(1,128)S(1)}, s32[1,32768]{1,0:T(1,128)}, u32[]{:S(2)}) copy-start(s32[1,32768]{1,0:T(1,128)} %param.22) | copy-start | bytes 393220
  0.0 12.9 %copy-start.7 = (s32[1,32768]{1,0:T(1,128)S(1)}, s32[1,32768]{1,0:T(1,128)}, u32[]{:S(2)}) copy-start(s32[1,32768]{1,0:T(1,128)} %param.21) | copy-start | bytes 393220
  0.0 32.2 %copy-start.4 = (f32[1,256,256]{2,1,0:T(8,128)S(1)}, f32[1,256,256]{2,1,0:T(8,128)}, u32[]{:S(2)}) copy-start(f32[1,256,256]{2,1,0:T(8,128)} %profile_ref.1) | copy-start | bytes 786436
  0.1 32.2 %copy-start.3 = (f32[256,256]{1,0:T(8,128)S(1)}, f32[256,256]{1,0:T(8,128)}, u32[]{:S(2)}) copy-start(f32[256,256]{1,0:T(8,128)} %velocity_ref.1) | copy-start | bytes 786436
  3.3 28.9 %collective-permute-start.1 = (f32[4,256,256]{2,1,0:T(8,128)}, f32[4,256,256]{2,1,0:T(8,128)S(1)}, u32[]{:S(2)}, u32[]{:S(2)}) collective-permute-start(f32[4,256,256]{2,1,0:T(8,128)} %get-tuple-element.21), channel_id=1, source_target_pairs={{1,0},{2,1},{3,2},{4,3},{5,4},{6,5},{7,6},{8,7},{9,8},{10,9},{11,1... | collective-permute-start | bytes 3145736 | tf_op jit(solution)/shard_map/ppermute | solution.py:642
  4.7 27.5 %collective-permute-start = (f32[4,256,256]{2,1,0:T(8,128)}, f32[4,256,256]{2,1,0:T(8,128)}, u32[]{:S(2)}, u32[]{:S(2)}) collective-permute-start(f32[4,256,256]{2,1,0:T(8,128)} %get-tuple-element.22), channel_id=1, source_target_pairs={{0,1},{1,2},{2,3},{3,4},{4,5},{5,6},{6,7},{7,8},{8,9},{9,10},{10,1... | collective-permute-start | bytes 3145736 | tf_op jit(solution)/shard_map/ppermute | solution.py:641
  7.8 24.4 %collective-permute-start.3 = (f32[4,256,256]{2,1,0:T(8,128)}, f32[4,256,256]{2,1,0:T(8,128)}, u32[]{:S(2)}, u32[]{:S(2)}) collective-permute-start(f32[4,256,256]{2,1,0:T(8,128)} %get-tuple-element.19), channel_id=1, source_target_pairs={{1,0},{2,1},{3,2},{4,3},{5,4},{6,5},{7,6},{8,7},{9,8},{10,9},{11,1... | collective-permute-start | bytes 3145736 | tf_op jit(solution)/shard_map/ppermute | solution.py:642
  12.2 20.0 %collective-permute-start.2 = (f32[4,256,256]{2,1,0:T(8,128)}, f32[4,256,256]{2,1,0:T(8,128)}, u32[]{:S(2)}, u32[]{:S(2)}) collective-permute-start(f32[4,256,256]{2,1,0:T(8,128)} %get-tuple-element.20), channel_id=1, source_target_pairs={{0,1},{1,2},{2,3},{3,4},{4,5},{5,6},{6,7},{7,8},{8,9},{9,10},{10,1... | collective-permute-start | bytes 3145736 | tf_op jit(solution)/shard_map/ppermute | solution.py:641
  32.3 2.2 %copy-start = (f32[16,256,256]{2,1,0:T(8,128)S(1)}, f32[16,256,256]{2,1,0:T(8,128)}, u32[]{:S(2)}) copy-start(f32[16,256,256]{2,1,0:T(8,128)} %rate_own.1) | copy-start | bytes 12582916
  34.5 2.2 %copy-start.2 = (f32[1,16,256,256]{3,2,1,0:T(8,128)S(1)}, f32[1,16,256,256]{3,2,1,0:T(8,128)}, u32[]{:S(2)}) copy-start(f32[1,16,256,256]{3,2,1,0:T(8,128)} %param.18) | copy-start | bytes 12582916
  36.6 52.0 %copy-start.14 = (f32[128]{0:T(128)S(1)}, f32[128]{0:T(128)}, u32[]{:S(2)}) copy-start(f32[128]{0:T(128)} %constant.50.clone) | copy-start | bytes 1540
  36.6 65.1 %copy-start.5 = (f32[128,128]{1,0:T(8,128)S(1)}, f32[128,128]{1,0:T(8,128)}, u32[]{:S(2)}) copy-start(f32[128,128]{1,0:T(8,128)} %constant.51.clone.table_ref) | copy-start | bytes 196612
  36.6 65.1 %copy-start.12 = (f32[128,1]{1,0:T(8,128)S(1)}, f32[128,1]{1,0:T(8,128)}, u32[]{:S(2)}) copy-start(f32[128,1]{1,0:T(8,128)} %constant.52.clone.symbol_depth) | copy-start | bytes 1540
  36.6 65.1 %copy-start.13 = (f32[1,128]{1,0:T(1,128)S(1)}, f32[1,128]{1,0:T(1,128)}, u32[]{:S(2)}) copy-start(f32[1,128]{1,0:T(1,128)} %constant.53.clone.symbol_rows) | copy-start | bytes 1540
  74.8 26.9 %all-to-all-start = ((f32[128,8,128]{2,1,0:T(8,128)}), f32[128,8,128]{2,1,0:T(8,128)S(1)}, u32[]{:S(2)}, u32[]{:S(2)}) async-start(f32[128,8,128]{2,1,0:T(8,128)} %bitcast.10), calls=%async_computation | async-start | bytes 1048576 | tf_op jit(solution)/shard_map/all_to_all | solution.py:667

commit v2 on v1

--- a/solution.py
+++ b/solution.py
@@ -39,12 +39,23 @@
     column_ref,
     step_ref,
     observed_ref,
+    rate,
+    state,
     keys_out,
     values_out,
     starts_out,
+    rate_near,
+    state_near,
     keys,
     values,
+    sems,
 ):
+    near = [
+        pltpu.make_async_copy(rate, rate_near, sems.at[0]),
+        pltpu.make_async_copy(state, state_near, sems.at[1]),
+    ]
+    for copy in near:
+        copy.start()
     offset = offset_ref[0]
     plane = (depth_ref[...] - (offset - LEAD)) & 255
     key = (plane << 17) | ((step_ref[...] - 1) << 16) | (row_ref[...] << 8) | column_ref[...]
@@ -165,30 +176,36 @@
         values_out[pl.ds(half, LANES, 2), :] = part.T
     keys_out[2 * LANES :, :] = jnp.full((8, LANES), -1, jnp.int32)
     values_out[2 * LANES :, :] = jnp.zeros((8, LANES), jnp.float32)
-
-
-def sort_probes(offset, depth, row, column, step_of, observed, planes):
+    for copy in near:
+        copy.wait()
+
+
+def sort_probes(offset, depth, row, column, step_of, observed, planes, rate, state):
     count = depth.size
     shape = (count // LANES, LANES)
     vmem = pl.BlockSpec(memory_space=pltpu.VMEM)
     smem = pl.BlockSpec(memory_space=pltpu.SMEM)
+    stay = pl.BlockSpec(memory_space=pl.ANY)
     return pl.pallas_call(
         sort_kernel,
         out_shape=(
             jax.ShapeDtypeStruct((shape[0] + 8, LANES), jnp.int32),
             jax.ShapeDtypeStruct((shape[0] + 8, LANES), jnp.float32),
             jax.ShapeDtypeStruct((planes + 1,), jnp.int32),
+            jax.ShapeDtypeStruct(rate.shape, jnp.float32),
+            jax.ShapeDtypeStruct(state.shape, jnp.float32),
         ),
-        in_specs=[smem] + [vmem] * 5,
-        out_specs=(vmem, vmem, smem),
+        in_specs=[smem] + [vmem] * 5 + [stay] * 2,
+        out_specs=(vmem, vmem, smem, stay, stay),
         scratch_shapes=[
             pltpu.VMEM((shape[0] // 8, 8, LANES), jnp.int32),
             pltpu.VMEM((shape[0] // 8, 8, LANES), jnp.float32),
+            pltpu.SemaphoreType.DMA((2,)),
         ],
-        compiler_params=pltpu.CompilerParams(vmem_limit_bytes=16 * 2**20),
+        compiler_params=pltpu.CompilerParams(vmem_limit_bytes=42 * 2**20),
         cost_estimate=pl.CostEstimate(flops=20_000_000, bytes_accessed=2**20, transcendentals=0),
         name="sort_probes",
-    )(offset, *(a.reshape(shape) for a in (depth, row, column, step_of, observed)))
+    )(offset, *(a.reshape(shape) for a in (depth, row, column, step_of, observed)), rate, state)
 
 
 def bin_kernel(starts, keys_ref, values_ref, *fields):
@@ -250,7 +267,7 @@
         in_specs=[pl.BlockSpec(memory_space=pltpu.SMEM), vmem, vmem],
         out_specs=(block,) * (2 * STEPS),
         compiler_params=pltpu.CompilerParams(
-            vmem_limit_bytes=8 * 2**20, dimension_semantics=("arbitrary",)
+            vmem_limit_bytes=5 * 2**20, dimension_semantics=("arbitrary",)
         ),
         cost_estimate=pl.CostEstimate(
             flops=30_000_000, bytes_accessed=20 * 2**20, transcendentals=0
@@ -548,7 +565,7 @@
             pltpu.VMEM((own // R, coarse, cols_count), jnp.float32),
         ],
         compiler_params=pltpu.CompilerParams(
-            vmem_limit_bytes=19 * 2**20, dimension_semantics=("arbitrary",)
+            vmem_limit_bytes=18 * 2**20, dimension_semantics=("arbitrary",)
         ),
         cost_estimate=pl.CostEstimate(
             flops=200_000_000, bytes_accessed=34 * 2**20, transcendentals=0
@@ -634,13 +651,44 @@
     )(received, jnp.asarray(hartley(received.shape[0])))
 
 
-def neighbours(array):
+def edges_kernel(rate, state, rate_first, rate_last, state_first, state_last, sems):
+    last = rate.shape[0] - HALO
+    copies = [
+        pltpu.make_async_copy(source.at[pl.ds(begin, HALO)], target, sems.at[at])
+        for at, (source, begin, target) in enumerate(
+            (
+                (rate, last, rate_last),
+                (rate, 0, rate_first),
+                (state, last, state_last),
+                (state, 0, state_first),
+            )
+        )
+    ]
+    for copy in copies:
+        copy.start()
+    for copy in copies:
+        copy.wait()
+
+
+def edges(rate, state):
+    stay = pl.BlockSpec(memory_space=pl.ANY)
+    end = jax.ShapeDtypeStruct((HALO, *rate.shape[1:]), jnp.float32)
+    return pl.pallas_call(
+        edges_kernel,
+        out_shape=(end,) * 4,
+        in_specs=[stay] * 2,
+        out_specs=(stay,) * 4,
+        scratch_shapes=[pltpu.SemaphoreType.DMA((4,))],
+        compiler_params=pltpu.CompilerParams(vmem_limit_bytes=60 * 2**20),
+        name="edges",
+    )(rate, state)
+
+
+def neighbours(first, last):
     count = lax.axis_size("domain")
     up = [(i, (i + 1) % count) for i in range(count)]
     down = [(j, i) for i, j in up]
-    before = lax.ppermute(array[-HALO:], "domain", up)
-    after = lax.ppermute(array[:HALO], "domain", down)
-    return before, array, after
+    return lax.ppermute(last, "domain", up), lax.ppermute(first, "domain", down)
 
 
 def local(log_rate, velocity, initial, profile, plane, depth, row, column, step_of, observed):
@@ -648,9 +696,10 @@
     domain_count, tracer_count = lax.axis_size("domain"), lax.axis_size("tracer")
     full = slab * domain_count
     offset = lax.axis_index("domain") * slab
-    rates = neighbours(log_rate)
-    states = neighbours(initial[0])
-    keys, values, starts = sort_probes(
+    rate_first, rate_last, state_first, state_last = edges(log_rate, initial[0])
+    rate_low, rate_high = neighbours(rate_first, rate_last)
+    state_low, state_high = neighbours(state_first, state_last)
+    keys, values, starts, rate_near, state_near = sort_probes(
         offset.astype(jnp.int32)[None],
         depth,
         row,
@@ -658,9 +707,13 @@
         step_of,
         observed,
         slab + 2 * LEAD,
+        log_rate,
+        initial[0],
     )
     source_plane = (plane - (offset - HALO)) % full
     fields = bin_probes(starts, keys, values, rows_count, cols_count)
+    rates = (rate_low, rate_near, rate_high)
+    states = (state_low, state_near, state_high)
     spectral = sweep(source_plane, rates, states, velocity, profile, fields)
     first, planes, second = rows_count // R, slab // R, cols_count // R
     axes = ("domain", "tracer")

time: 118 us -> 236 us (2.00)
  Pallas kernels: 60 us -> 184 us
  local copies, waits for them, and re-layouts: 9.72 us -> 4.28 us
    pallas_call x0 -> x1, Pallas kernels: none -> 128 us  [edges(): pl.pallas_call(edges_kernel, out_shape=(end,) * 4, in_specs=[stay] * 2, o...]
    slice x2 -> x0, local copies, waits for them, and re-layouts: 4.71 us -> none  [neighbours(): after = lax.ppermute(array[:HALO], 'domain', down)]
    pallas_call x1, Pallas kernels: 38.2 us -> 35.2 us  [sweep(): pl.pallas_call(sweep_kernel, grid=(total,), out_shape=jax.ShapeDtypeStruc...]
  transfers between devices with their start and end apart: 5 -> 5, of which waited for: 1 -> 1; matrix products, arithmetic and copies ran while one was open for 2% -> 0% of each run, Pallas kernels for 16% -> 8%
where the time goes in v2:
time: 236 us; the launch traced here: 235 us
  Pallas kernels  184 us (78%)
  starting transfers between devices  19.2 us (8%)
  blocking collectives  13.9 us (6%)
  waiting for transfers between devices  12.6 us (5%)
  local copies, waits for them, and re-layouts  4.28 us (2%)
    pallas_call x1, Pallas kernels, edges(): pl.pallas_call(edges_kernel, out_shape=(end,) * 4, in_specs=[stay] * 2, o...  128 us
    pallas_call x1, Pallas kernels, sweep(): pl.pallas_call(sweep_kernel, grid=(total,), out_shape=jax.ShapeDtypeStruc...  35.2 us
    all_to_all x1, blocking collectives, local(): result = lax.all_to_all(back, axes, split_axis=0, concat_axis=0, tiled=True)  13.9 us
    all_to_all x1, waiting for transfers between devices, local(): lax.all_to_all(spectral.reshape(second, planes, first), axes, split_axis=...  12.6 us
    all_to_all x1, starting transfers between devices, local(): lax.all_to_all(spectral.reshape(second, planes, first), axes, split_axis=...  11.6 us
    pallas_call x1, Pallas kernels, bin_probes(): pl.pallas_call(bin_kernel, grid=(places,), out_shape=(field,) * (2 * STEP...  9.21 us
    pallas_call x1, Pallas kernels, sort_probes(): pl.pallas_call(sort_kernel, out_shape=(jax.ShapeDtypeStruct((shape[0] + 8...  9.09 us
    ppermute x2, starting transfers between devices, neighbours(): lax.ppermute(last, 'domain', up)  4.84 us
  transfers between devices with their start and end apart: 5, of which 1 were waited for; matrix products, arithmetic and copies ran while one was open for 0% of the time, Pallas kernels for 8%

profile of v2, /device:TPU:1, one launch (start us, length us, event | category | flops | bytes accessed | tf_op | source)
XLA Modules:
  0.0 235.1 jit_solution(17110224067297029990)
XLA Ops:
  0.0 128.2 %edges.1 = (f32[4,256,256]{2,1,0:T(8,128)}, f32[4,256,256]{2,1,0:T(8,128)}, f32[4,256,256]{2,1,0:T(8,128)}, f32[4,256,256]{2,1,0:T(8,128)}) custom-call(f32[16,256,256]{2,1,0:T(8,128)} %rate.3, f32[16,256,256]{2,1,0:T(8,128)} %bitcast.23), custom_call_target="tpu_custom_call" | custom-call | tf_op jit(solution)/shard_map/edges/pallas_call | solution.py:676
  128.2 0.0 copy-start
  128.2 3.1 %collective-permute-start = (f32[4,256,256]{2,1,0:T(8,128)}, f32[4,256,256]{2,1,0:T(8,128)S(1)}, u32[]{:S(2)}, u32[]{:S(2)}) collective-permute-start(f32[4,256,256]{2,1,0:T(8,128)} %get-tuple-element.18), channel_id=1, source_target_pairs={{0,1},{1,2},{2,3},{3,4},{4,5},{5,6},{6,7},{7,8},{8,9},{9,10},{10,1... | collective-permute-start | bytes 3145736 | tf_op jit(solution)/shard_map/ppermute | solution.py:691
  131.3 0.0 collective-permute-start.1
  131.3 1.7 collective-permute-start.2
  133.1 2.8 %collective-permute-start.3 = (f32[4,256,256]{2,1,0:T(8,128)}, f32[4,256,256]{2,1,0:T(8,128)}, u32[]{:S(2)}, u32[]{:S(2)}) collective-permute-start(f32[4,256,256]{2,1,0:T(8,128)} %get-tuple-element.23), channel_id=1, source_target_pairs={{1,0},{2,1},{3,2},{4,3},{5,4},{6,5},{7,6},{8,7},{9,8},{10,9},{11,1... | collective-permute-start | bytes 3145736 | tf_op jit(solution)/shard_map/ppermute | solution.py:691
  136.5 0.0 copy-start.1
  136.5 0.0 copy-done.3
  136.5 0.0 copy-start.4
  136.5 0.9 copy-done.4
  137.4 0.9 copy-done.5
  138.4 0.9 copy-done.6
  139.3 0.9 copy-done.7
  140.2 9.1 %sort_probes.1 = (s32[264,128]{1,0:T(8,128)S(1)}, f32[264,128]{1,0:T(8,128)S(1)}, s32[21]{0:T(128)S(1)}, f32[16,256,256]{2,1,0:T(8,128)S(1)}, f32[16,256,256]{2,1,0:T(8,128)S(1)}) custom-call(s32[1]{0:T(128)} %bitcast.2.offset_ref, s32[256,128]{1,0:T(8,128)S(1)} %bitcast.18, s32[256,128]{1,0:T(8,128)S(1)} %bitcast.19, s32[256,128]{1,0:T(8,128)S(1)} %bitcast.20, ...), custom_call_target="tpu_custom_call" | custom-call | flops 20000000 | bytes 1048576 | tf_op jit(solution)/shard_map/sort_probes/pallas_call | solution.py:189
  149.3 9.2 %bin_probes.1 = (f32[20,256,256]{2,1,0:T(8,128)S(1)}, f32[20,256,256]{2,1,0:T(8,128)S(1)}, f32[20,256,256]{2,1,0:T(8,128)S(1)}, f32[20,256,256]{2,1,0:T(8,128)S(1)}) custom-call(s32[21]{0:T(128)S(1)} %get-tuple-element.24.starts, s32[264,128]{1,0:T(8,128)S(1)} %get-tuple-element.25.keys_ref, f32[264,128]{1,0:T(8,128)S(1)} %get-tuple-element.26.values_ref), custom_call_target="tpu_custom_call" | custom-call | flops 30000000 | bytes 20971520 | tf_op jit(solution)/shard_map/bin_probes/pallas_call | solution.py:263
  158.5 0.0 collective-permute-done.rate_low
  158.5 0.0 collective-permute-done.1.rate_high
  158.5 0.0 collective-permute-done.2.state_low
  158.5 0.0 collective-permute-done.3.state_high
  158.5 0.0 copy-done
  158.5 0.0 copy-done.1
  158.6 0.0 copy-start.11
  158.6 0.0 copy-start.2
  158.6 0.0 copy-start.9
  158.6 0.0 copy-start.10
  158.6 35.2 %sweep.1 = f32[1024,128]{1,0:T(8,128)} custom-call(s32[1]{0:T(128)S(6)} %select_n.11.source_plane, f32[4,256,256]{2,1,0:T(8,128)S(1)} %collective-permute-done.rate_low, f32[16,256,256]{2,1,0:T(8,128)S(1)} %get-tuple-element.19.rate_own, f32[4,256,256]{2,1,0:T(8,128)S(1)} %collective-permute-done.1.rate_high, ...), custom_call_target="tpu_custom_call" | custom-call | flops 200000000 | bytes 35651584 | tf_op jit(solution)/shard_map/sweep/pallas_call | solution.py:553
  193.8 11.6 %all-to-all-start = ((f32[128,8,128]{2,1,0:T(8,128)}), f32[128,8,128]{2,1,0:T(8,128)S(1)}, u32[]{:S(2)}, u32[]{:S(2)}) async-start(f32[128,8,128]{2,1,0:T(8,128)} %bitcast.8), calls=%async_computation | async-start | bytes 1048576 | tf_op jit(solution)/shard_map/all_to_all | solution.py:720
  205.5 0.6 dynamic_slice.3.lam_second
  206.0 12.6 %all-to-all-done = f32[128,8,128]{2,1,0:T(8,128)S(1)} async-done(((f32[128,8,128]{2,1,0:T(8,128)}), f32[128,8,128]{2,1,0:T(8,128)S(1)}, u32[]{:S(2)}, u32[]{:S(2)}) %all-to-all-start) | async-done | bytes 524320 | tf_op jit(solution)/shard_map/all_to_all | solution.py:720
  218.6 1.7 filter.1
  220.3 13.9 %all_to_all.16 = f32[128,1,128]{2,1,0:T(1,128)S(1)} all-to-all(f32[128,1,128]{2,1,0:T(1,128)S(1)} %bitcast.17), channel_id=1, replica_groups=mesh['tracer'=8,'domain'=16] {'domain','tracer'}, dimensions={0} | all-to-all | bytes 131072 | tf_op jit(solution)/shard_map/all_to_all | solution.py:726
  234.2 0.9 inverse_columns.1
  (10 shorter events, 0.0 us)
Async XLA Ops:
  0.0 136.5 %copy-start.3 = (s32[1,32768]{1,0:T(1,128)S(1)}, s32[1,32768]{1,0:T(1,128)}, u32[]{:S(2)}) copy-start(s32[1,32768]{1,0:T(1,128)} %param.21) | copy-start | bytes 393220
  128.2 30.3 %copy-start = (f32[256,256]{1,0:T(8,128)S(1)}, f32[256,256]{1,0:T(8,128)}, u32[]{:S(2)}) copy-start(f32[256,256]{1,0:T(8,128)} %velocity_ref.1) | copy-start | bytes 786436
  128.2 30.3 %collective-permute-start = (f32[4,256,256]{2,1,0:T(8,128)}, f32[4,256,256]{2,1,0:T(8,128)S(1)}, u32[]{:S(2)}, u32[]{:S(2)}) collective-permute-start(f32[4,256,256]{2,1,0:T(8,128)} %get-tuple-element.18), channel_id=1, source_target_pairs={{0,1},{1,2},{2,3},{3,4},{4,5},{5,6},{6,7},{7,8},{8,9},{9,10},{10,1... | collective-permute-start | bytes 3145736 | tf_op jit(solution)/shard_map/ppermute | solution.py:691
  131.3 27.2 %collective-permute-start.1 = (f32[4,256,256]{2,1,0:T(8,128)}, f32[4,256,256]{2,1,0:T(8,128)S(1)}, u32[]{:S(2)}, u32[]{:S(2)}) collective-permute-start(f32[4,256,256]{2,1,0:T(8,128)} %get-tuple-element.20), channel_id=1, source_target_pairs={{1,0},{2,1},{3,2},{4,3},{5,4},{6,5},{7,6},{8,7},{9,8},{10,9},{11,1... | collective-permute-start | bytes 3145736 | tf_op jit(solution)/shard_map/ppermute | solution.py:691
  131.3 27.2 %collective-permute-start.2 = (f32[4,256,256]{2,1,0:T(8,128)}, f32[4,256,256]{2,1,0:T(8,128)S(1)}, u32[]{:S(2)}, u32[]{:S(2)}) collective-permute-start(f32[4,256,256]{2,1,0:T(8,128)} %get-tuple-element.21), channel_id=1, source_target_pairs={{0,1},{1,2},{2,3},{3,4},{4,5},{5,6},{6,7},{7,8},{8,9},{9,10},{10,1... | collective-permute-start | bytes 3145736 | tf_op jit(solution)/shard_map/ppermute | solution.py:691
  133.1 25.5 %collective-permute-start.3 = (f32[4,256,256]{2,1,0:T(8,128)}, f32[4,256,256]{2,1,0:T(8,128)}, u32[]{:S(2)}, u32[]{:S(2)}) collective-permute-start(f32[4,256,256]{2,1,0:T(8,128)} %get-tuple-element.23), channel_id=1, source_target_pairs={{1,0},{2,1},{3,2},{4,3},{5,4},{6,5},{7,6},{8,7},{9,8},{10,9},{11,1... | collective-permute-start | bytes 3145736 | tf_op jit(solution)/shard_map/ppermute | solution.py:691
  136.5 22.1 %copy-start.1 = (f32[1,256,256]{2,1,0:T(8,128)S(1)}, f32[1,256,256]{2,1,0:T(8,128)}, u32[]{:S(2)}) copy-start(f32[1,256,256]{2,1,0:T(8,128)} %profile_ref.1) | copy-start | bytes 786436
  136.5 0.9 copy-start.4
  137.4 0.9 copy-start.5
  138.3 0.9 copy-start.6
  139.3 0.9 copy-start.7
  140.2 18.4 %copy-start.8 = (f32[128,256]{1,0:T(8,128)S(1)}, f32[128,256]{1,0:T(8,128)}, u32[]{:S(2)}) copy-start(f32[128,256]{1,0:T(8,128)} %constant.49.clone.columns_table) | copy-start | bytes 393220
  158.6 46.9 %copy-start.11 = (f32[128]{0:T(128)S(1)}, f32[128]{0:T(128)}, u32[]{:S(2)}) copy-start(f32[128]{0:T(128)} %constant.50.clone) | copy-start | bytes 1540
  158.6 60.0 %copy-start.2 = (f32[128,128]{1,0:T(8,128)S(1)}, f32[128,128]{1,0:T(8,128)}, u32[]{:S(2)}) copy-start(f32[128,128]{1,0:T(8,128)} %constant.51.clone.table_ref) | copy-start | bytes 196612
  158.6 60.0 %copy-start.9 = (f32[128,1]{1,0:T(8,128)S(1)}, f32[128,1]{1,0:T(8,128)}, u32[]{:S(2)}) copy-start(f32[128,1]{1,0:T(8,128)} %constant.52.clone.symbol_depth) | copy-start | bytes 1540
  158.6 60.0 %copy-start.10 = (f32[1,128]{1,0:T(1,128)S(1)}, f32[1,128]{1,0:T(1,128)}, u32[]{:S(2)}) copy-start(f32[1,128]{1,0:T(1,128)} %constant.53.clone.symbol_rows) | copy-start | bytes 1540
  193.8 24.8 %all-to-all-start = ((f32[128,8,128]{2,1,0:T(8,128)}), f32[128,8,128]{2,1,0:T(8,128)S(1)}, u32[]{:S(2)}, u32[]{:S(2)}) async-start(f32[128,8,128]{2,1,0:T(8,128)} %bitcast.8), calls=%async_computation | async-start | bytes 1048576 | tf_op jit(solution)/shard_map/all_to_all | solution.py:720

commit v3 on v2

--- a/solution.py
+++ b/solution.py
@@ -651,39 +651,6 @@
     )(received, jnp.asarray(hartley(received.shape[0])))
 
 
-def edges_kernel(rate, state, rate_first, rate_last, state_first, state_last, sems):
-    last = rate.shape[0] - HALO
-    copies = [
-        pltpu.make_async_copy(source.at[pl.ds(begin, HALO)], target, sems.at[at])
-        for at, (source, begin, target) in enumerate(
-            (
-                (rate, last, rate_last),
-                (rate, 0, rate_first),
-                (state, last, state_last),
-                (state, 0, state_first),
-            )
-        )
-    ]
-    for copy in copies:
-        copy.start()
-    for copy in copies:
-        copy.wait()
-
-
-def edges(rate, state):
-    stay = pl.BlockSpec(memory_space=pl.ANY)
-    end = jax.ShapeDtypeStruct((HALO, *rate.shape[1:]), jnp.float32)
-    return pl.pallas_call(
-        edges_kernel,
-        out_shape=(end,) * 4,
-        in_specs=[stay] * 2,
-        out_specs=(stay,) * 4,
-        scratch_shapes=[pltpu.SemaphoreType.DMA((4,))],
-        compiler_params=pltpu.CompilerParams(vmem_limit_bytes=60 * 2**20),
-        name="edges",
-    )(rate, state)
-
-
 def neighbours(first, last):
     count = lax.axis_size("domain")
     up = [(i, (i + 1) % count) for i in range(count)]
@@ -696,9 +663,8 @@
     domain_count, tracer_count = lax.axis_size("domain"), lax.axis_size("tracer")
     full = slab * domain_count
     offset = lax.axis_index("domain") * slab
-    rate_first, rate_last, state_first, state_last = edges(log_rate, initial[0])
-    rate_low, rate_high = neighbours(rate_first, rate_last)
-    state_low, state_high = neighbours(state_first, state_last)
+    rate_low, rate_high = neighbours(log_rate[:HALO], log_rate[-HALO:])
+    state_low, state_high = neighbours(initial[0, :HALO], initial[0, -HALO:])
     keys, values, starts, rate_near, state_near = sort_probes(
         offset.astype(jnp.int32)[None],
         depth,

time: 236 us -> 115 us (0.49)
  Pallas kernels: 184 us -> 58.5 us
  local copies, waits for them, and re-layouts: 4.28 us -> 7.08 us
    pallas_call x1 -> x0, Pallas kernels: 128 us -> none  [edges(): pl.pallas_call(edges_kernel, out_shape=(end,) * 4, in_specs=[stay] * 2, o...]
    ppermute x2, starting transfers between devices: 4.84 us -> 1.62 us  [neighbours(): lax.ppermute(last, 'domain', up)]
    slice x0 -> x1, local copies, waits for them, and re-layouts: none -> 3.14 us  [local(): rate_low, rate_high = neighbours(log_rate[:HALO], log_rate[-HALO:])]
    ppermute x2, starting transfers between devices: 2.76 us -> 5.82 us  [neighbours(): lax.ppermute(first, 'domain', down)]
    all_to_all x1, starting transfers between devices: 11.6 us -> 14 us  [local(): lax.all_to_all(spectral.reshape(second, planes, first), axes, split_axis=...]
  transfers between devices with their start and end apart: 5 -> 5, of which waited for: 1 -> 1; matrix products, arithmetic and copies ran while one was open for 0% -> 2% of each run, Pallas kernels for 8% -> 17%
where the time goes in v3:
time: 115 us; the launch traced here: 114 us
  Pallas kernels  58.5 us (51%)
  starting transfers between devices  21.5 us (19%)
  blocking collectives  13.9 us (12%)
  waiting for transfers between devices  12.6 us (11%)
  local copies, waits for them, and re-layouts  7.08 us (6%)
    pallas_call x1, Pallas kernels, sweep(): pl.pallas_call(sweep_kernel, grid=(total,), out_shape=jax.ShapeDtypeStruc...  36.8 us
    all_to_all x1, starting transfers between devices, local(): lax.all_to_all(spectral.reshape(second, planes, first), axes, split_axis=...  14 us
    all_to_all x1, blocking collectives, local(): result = lax.all_to_all(back, axes, split_axis=0, concat_axis=0, tiled=True)  13.9 us
    all_to_all x1, waiting for transfers between devices, local(): lax.all_to_all(spectral.reshape(second, planes, first), axes, split_axis=...  12.6 us
    pallas_call x1, Pallas kernels, bin_probes(): pl.pallas_call(bin_kernel, grid=(places,), out_shape=(field,) * (2 * STEP...  10 us
    pallas_call x1, Pallas kernels, sort_probes(): pl.pallas_call(sort_kernel, out_shape=(jax.ShapeDtypeStruct((shape[0] + 8...  9.09 us
    ppermute x2, starting transfers between devices, neighbours(): lax.ppermute(first, 'domain', down)  5.82 us
    slice x1, local copies, waits for them, and re-layouts, local(): rate_low, rate_high = neighbours(log_rate[:HALO], log_rate[-HALO:])  3.14 us
  transfers between devices with their start and end apart: 5, of which 1 were waited for; matrix products, arithmetic and copies ran while one was open for 2% of the time, Pallas kernels for 17%

profile of v3, /device:TPU:1, one launch (start us, length us, event | category | flops | bytes accessed | tf_op | source)
XLA Modules:
  0.0 114.4 jit_solution(12765318771822036246)
XLA Ops:
  0.0 0.0 copy-start.3
  0.0 3.1 %fusion = (f32[4,256,256]{2,1,0:T(8,128)}, f32[4,256,256]{2,1,0:T(8,128)}) fusion(f32[16,256,256]{2,1,0:T(8,128)} %rate.1), kind=kLoop, calls=%fused_computation.2 | loop fusion | bytes 4194304 | tf_op jit(solution)/shard_map/slice | solution.py:666
  3.2 1.4 %collective-permute-start.1 = (f32[4,256,256]{2,1,0:T(8,128)}, f32[4,256,256]{2,1,0:T(8,128)S(1)}, u32[]{:S(2)}, u32[]{:S(2)}) collective-permute-start(f32[4,256,256]{2,1,0:T(8,128)} %get-tuple-element.25), channel_id=1, source_target_pairs={{1,0},{2,1},{3,2},{4,3},{5,4},{6,5},{7,6},{8,7},{9,8},{10,9},{11,1... | collective-permute-start | bytes 3145736 | tf_op jit(solution)/shard_map/ppermute | solution.py:658
  4.6 1.6 %collective-permute-start = (f32[4,256,256]{2,1,0:T(8,128)}, f32[4,256,256]{2,1,0:T(8,128)S(1)}, u32[]{:S(2)}, u32[]{:S(2)}) collective-permute-start(f32[4,256,256]{2,1,0:T(8,128)} %get-tuple-element.26), channel_id=1, source_target_pairs={{0,1},{1,2},{2,3},{3,4},{4,5},{5,6},{6,7},{7,8},{8,9},{9,10},{10,1... | collective-permute-start | bytes 3145736 | tf_op jit(solution)/shard_map/ppermute | solution.py:658
  6.2 0.0 copy-done.11
  6.2 1.5 %slice_bitcast_fusion = (f32[4,256,256]{2,1,0:T(8,128)}, f32[4,256,256]{2,1,0:T(8,128)}) fusion(f32[1,16,256,256]{3,2,1,0:T(8,128)S(1)} %copy-done.11), kind=kLoop, calls=%fused_computation | loop fusion | bytes 4194304 | tf_op jit(solution)/shard_map/squeeze | solution.py:667
  7.7 4.4 %collective-permute-start.3 = (f32[4,256,256]{2,1,0:T(8,128)}, f32[4,256,256]{2,1,0:T(8,128)S(1)}, u32[]{:S(2)}, u32[]{:S(2)}) collective-permute-start(f32[4,256,256]{2,1,0:T(8,128)} %get-tuple-element.23), channel_id=1, source_target_pairs={{1,0},{2,1},{3,2},{4,3},{5,4},{6,5},{7,6},{8,7},{9,8},{10,9},{11,1... | collective-permute-start | bytes 3145736 | tf_op jit(solution)/shard_map/ppermute | solution.py:658
  12.1 0.0 collective-permute-start.2
  12.8 0.0 copy-done.5
  12.8 0.0 copy-done.4
  12.8 0.0 copy-done.3
  12.8 0.0 copy-start.6
  12.8 0.9 copy-done.6
  13.7 0.9 copy-done.7
  14.6 9.1 %sort_probes.1 = (s32[264,128]{1,0:T(8,128)S(1)}, f32[264,128]{1,0:T(8,128)S(1)}, s32[21]{0:T(128)S(1)}, f32[16,256,256]{2,1,0:T(8,128)S(1)}, f32[16,256,256]{2,1,0:T(8,128)S(1)}) custom-call(s32[1]{0:T(128)} %bitcast.1.offset_ref, s32[256,128]{1,0:T(8,128)S(1)} %bitcast.22, s32[256,128]{1,0:T(8,128)S(1)} %bitcast.23, s32[256,128]{1,0:T(8,128)S(1)} %bitcast.24, ...), custom_call_target="tpu_custom_call" | custom-call | flops 20000000 | bytes 1048576 | tf_op jit(solution)/shard_map/sort_probes/pallas_call | solution.py:189
  23.7 10.0 %bin_probes.1 = (f32[20,256,256]{2,1,0:T(8,128)S(1)}, f32[20,256,256]{2,1,0:T(8,128)S(1)}, f32[20,256,256]{2,1,0:T(8,128)S(1)}, f32[20,256,256]{2,1,0:T(8,128)S(1)}) custom-call(s32[21]{0:T(128)S(1)} %get-tuple-element.16.starts, s32[264,128]{1,0:T(8,128)S(1)} %get-tuple-element.17.keys_ref, f32[264,128]{1,0:T(8,128)S(1)} %get-tuple-element.18.values_ref), custom_call_target="tpu_custom_call" | custom-call | flops 30000000 | bytes 20971520 | tf_op jit(solution)/shard_map/bin_probes/pallas_call | solution.py:263
  33.8 0.0 collective-permute-done.1.rate_high
  33.8 0.0 collective-permute-done.rate_low
  33.8 0.0 collective-permute-done.3.state_high
  33.8 0.0 collective-permute-done.2.state_low
  33.8 0.0 copy-done
  33.9 0.0 copy-start.12
  33.9 0.0 copy-start.2
  33.9 0.0 copy-start.9
  33.9 0.0 copy-start.10
  33.9 36.8 %sweep.1 = f32[1024,128]{1,0:T(8,128)} custom-call(s32[1]{0:T(128)S(6)} %select_n.11.source_plane, f32[4,256,256]{2,1,0:T(8,128)S(1)} %collective-permute-done.rate_low, f32[16,256,256]{2,1,0:T(8,128)S(1)} %get-tuple-element.14.rate_own, f32[4,256,256]{2,1,0:T(8,128)S(1)} %collective-permute-done.1.rate_high, ...), custom_call_target="tpu_custom_call" | custom-call | flops 200000000 | bytes 35651584 | tf_op jit(solution)/shard_map/sweep/pallas_call | solution.py:553
  70.7 14.0 %all-to-all-start = ((f32[128,8,128]{2,1,0:T(8,128)}), f32[128,8,128]{2,1,0:T(8,128)S(1)}, u32[]{:S(2)}, u32[]{:S(2)}) async-start(f32[128,8,128]{2,1,0:T(8,128)} %bitcast.10), calls=%async_computation | async-start | bytes 1048576 | tf_op jit(solution)/shard_map/all_to_all | solution.py:686
  84.7 0.6 dynamic_slice.3.lam_second
  85.3 12.6 %all-to-all-done = f32[128,8,128]{2,1,0:T(8,128)S(1)} async-done(((f32[128,8,128]{2,1,0:T(8,128)}), f32[128,8,128]{2,1,0:T(8,128)S(1)}, u32[]{:S(2)}, u32[]{:S(2)}) %all-to-all-start) | async-done | bytes 524320 | tf_op jit(solution)/shard_map/all_to_all | solution.py:686
  97.9 1.7 %filter.1 = f32[128,128]{1,0:T(8,128)S(1)} custom-call(f32[1]{0:T(128)} %dynamic_slice.3.lam_second, f32[16,8,8,128]{3,2,1,0:T(8,128)S(1)} %bitcast.19, f32[128,128]{1,0:T(8,128)S(1)} %copy-done.2, f32[128,1]{1,0:T(8,128)S(1)} %copy-done.9, f32[1,128]{1,0:T(1,128)S(1)} %copy-done.10), custom_call_target="tpu_custom_call" | custom-call | tf_op jit(solution)/shard_map/filter/pallas_call | solution.py:615
  99.6 13.9 %all_to_all.16 = f32[128,1,128]{2,1,0:T(1,128)S(1)} all-to-all(f32[128,1,128]{2,1,0:T(1,128)S(1)} %bitcast.21), channel_id=1, replica_groups=mesh['tracer'=8,'domain'=16] {'domain','tracer'}, dimensions={0} | all-to-all | bytes 131072 | tf_op jit(solution)/shard_map/all_to_all | solution.py:692
  113.5 0.9 inverse_columns.1
  (13 shorter events, 0.0 us)
Async XLA Ops:
  0.0 6.2 %copy-start.11 = (f32[1,16,256,256]{3,2,1,0:T(8,128)S(1)}, f32[1,16,256,256]{3,2,1,0:T(8,128)}, u32[]{:S(2)}) copy-start(f32[1,16,256,256]{3,2,1,0:T(8,128)} %param.18) | copy-start | bytes 12582916
  0.0 12.8 %copy-start.5 = (s32[1,32768]{1,0:T(1,128)S(1)}, s32[1,32768]{1,0:T(1,128)}, u32[]{:S(2)}) copy-start(s32[1,32768]{1,0:T(1,128)} %param.23) | copy-start | bytes 393220
  0.0 12.8 %copy-start.4 = (s32[1,32768]{1,0:T(1,128)S(1)}, s32[1,32768]{1,0:T(1,128)}, u32[]{:S(2)}) copy-start(s32[1,32768]{1,0:T(1,128)} %param.22) | copy-start | bytes 393220
  0.0 12.8 %copy-start.3 = (s32[1,32768]{1,0:T(1,128)S(1)}, s32[1,32768]{1,0:T(1,128)}, u32[]{:S(2)}) copy-start(s32[1,32768]{1,0:T(1,128)} %param.21) | copy-start | bytes 393220
  3.2 30.6 %collective-permute-start.1 = (f32[4,256,256]{2,1,0:T(8,128)}, f32[4,256,256]{2,1,0:T(8,128)S(1)}, u32[]{:S(2)}, u32[]{:S(2)}) collective-permute-start(f32[4,256,256]{2,1,0:T(8,128)} %get-tuple-element.25), channel_id=1, source_target_pairs={{1,0},{2,1},{3,2},{4,3},{5,4},{6,5},{7,6},{8,7},{9,8},{10,9},{11,1... | collective-permute-start | bytes 3145736 | tf_op jit(solution)/shard_map/ppermute | solution.py:658
  4.6 29.2 %collective-permute-start = (f32[4,256,256]{2,1,0:T(8,128)}, f32[4,256,256]{2,1,0:T(8,128)S(1)}, u32[]{:S(2)}, u32[]{:S(2)}) collective-permute-start(f32[4,256,256]{2,1,0:T(8,128)} %get-tuple-element.26), channel_id=1, source_target_pairs={{0,1},{1,2},{2,3},{3,4},{4,5},{5,6},{6,7},{7,8},{8,9},{9,10},{10,1... | collective-permute-start | bytes 3145736 | tf_op jit(solution)/shard_map/ppermute | solution.py:658
  7.7 26.1 %collective-permute-start.3 = (f32[4,256,256]{2,1,0:T(8,128)}, f32[4,256,256]{2,1,0:T(8,128)S(1)}, u32[]{:S(2)}, u32[]{:S(2)}) collective-permute-start(f32[4,256,256]{2,1,0:T(8,128)} %get-tuple-element.23), channel_id=1, source_target_pairs={{1,0},{2,1},{3,2},{4,3},{5,4},{6,5},{7,6},{8,7},{9,8},{10,9},{11,1... | collective-permute-start | bytes 3145736 | tf_op jit(solution)/shard_map/ppermute | solution.py:658
  12.1 21.7 %collective-permute-start.2 = (f32[4,256,256]{2,1,0:T(8,128)}, f32[4,256,256]{2,1,0:T(8,128)}, u32[]{:S(2)}, u32[]{:S(2)}) collective-permute-start(f32[4,256,256]{2,1,0:T(8,128)} %get-tuple-element.24), channel_id=1, source_target_pairs={{0,1},{1,2},{2,3},{3,4},{4,5},{5,6},{6,7},{7,8},{8,9},{9,10},{10,1... | collective-permute-start | bytes 3145736 | tf_op jit(solution)/shard_map/ppermute | solution.py:658
  12.8 0.9 copy-start.6
  13.7 0.9 copy-start.7
  14.6 19.2 %copy-start = (f32[256,256]{1,0:T(8,128)S(1)}, f32[256,256]{1,0:T(8,128)}, u32[]{:S(2)}) copy-start(f32[256,256]{1,0:T(8,128)} %velocity_ref.1) | copy-start | bytes 786436
  14.6 19.2 %copy-start.1 = (f32[1,256,256]{2,1,0:T(8,128)S(1)}, f32[1,256,256]{2,1,0:T(8,128)}, u32[]{:S(2)}) copy-start(f32[1,256,256]{2,1,0:T(8,128)} %profile_ref.1) | copy-start | bytes 786436
  14.6 19.2 %copy-start.8 = (f32[128,256]{1,0:T(8,128)S(1)}, f32[128,256]{1,0:T(8,128)}, u32[]{:S(2)}) copy-start(f32[128,256]{1,0:T(8,128)} %constant.49.clone.columns_table) | copy-start | bytes 393220
  33.9 50.9 %copy-start.12 = (f32[128]{0:T(128)S(1)}, f32[128]{0:T(128)}, u32[]{:S(2)}) copy-start(f32[128]{0:T(128)} %constant.50.clone) | copy-start | bytes 1540
  33.9 64.0 %copy-start.2 = (f32[128,128]{1,0:T(8,128)S(1)}, f32[128,128]{1,0:T(8,128)}, u32[]{:S(2)}) copy-start(f32[128,128]{1,0:T(8,128)} %constant.51.clone.table_ref) | copy-start | bytes 196612
  33.9 64.0 %copy-start.9 = (f32[128,1]{1,0:T(8,128)S(1)}, f32[128,1]{1,0:T(8,128)}, u32[]{:S(2)}) copy-start(f32[128,1]{1,0:T(8,128)} %constant.52.clone.symbol_depth) | copy-start | bytes 1540
  33.9 64.0 %copy-start.10 = (f32[1,128]{1,0:T(1,128)S(1)}, f32[1,128]{1,0:T(1,128)}, u32[]{:S(2)}) copy-start(f32[1,128]{1,0:T(1,128)} %constant.53.clone.symbol_rows) | copy-start | bytes 1540
  70.7 27.2 %all-to-all-start = ((f32[128,8,128]{2,1,0:T(8,128)}), f32[128,8,128]{2,1,0:T(8,128)S(1)}, u32[]{:S(2)}, u32[]{:S(2)}) async-start(f32[128,8,128]{2,1,0:T(8,128)} %bitcast.10), calls=%async_computation | async-start | bytes 1048576 | tf_op jit(solution)/shard_map/all_to_all | solution.py:686

commit v4 on v3

--- a/solution.py
+++ b/solution.py
@@ -34,11 +34,11 @@
 
 def sort_kernel(
     offset_ref,
-    depth_ref,
-    row_ref,
-    column_ref,
-    step_ref,
-    observed_ref,
+    depth_far,
+    row_far,
+    column_far,
+    step_far,
+    observed_far,
     rate,
     state,
     keys_out,
@@ -48,14 +48,35 @@
     state_near,
     keys,
     values,
+    depth_ref,
+    row_ref,
+    column_ref,
+    step_ref,
+    observed_ref,
     sems,
 ):
+    probes = [
+        pltpu.make_async_copy(far, near, sems.at[2 + at])
+        for at, (far, near) in enumerate(
+            (
+                (depth_far, depth_ref),
+                (row_far, row_ref),
+                (column_far, column_ref),
+                (step_far, step_ref),
+                (observed_far, observed_ref),
+            )
+        )
+    ]
+    for copy in probes:
+        copy.start()
     near = [
         pltpu.make_async_copy(rate, rate_near, sems.at[0]),
         pltpu.make_async_copy(state, state_near, sems.at[1]),
     ]
     for copy in near:
         copy.start()
+    for copy in probes:
+        copy.wait()
     offset = offset_ref[0]
     plane = (depth_ref[...] - (offset - LEAD)) & 255
     key = (plane << 17) | ((step_ref[...] - 1) << 16) | (row_ref[...] << 8) | column_ref[...]
@@ -195,12 +216,14 @@
             jax.ShapeDtypeStruct(rate.shape, jnp.float32),
             jax.ShapeDtypeStruct(state.shape, jnp.float32),
         ),
-        in_specs=[smem] + [vmem] * 5 + [stay] * 2,
+        in_specs=[smem] + [stay] * 7,
         out_specs=(vmem, vmem, smem, stay, stay),
         scratch_shapes=[
             pltpu.VMEM((shape[0] // 8, 8, LANES), jnp.int32),
             pltpu.VMEM((shape[0] // 8, 8, LANES), jnp.float32),
-            pltpu.SemaphoreType.DMA((2,)),
+            *[pltpu.VMEM(shape, jnp.int32)] * 4,
+            pltpu.VMEM(shape, jnp.float32),
+            pltpu.SemaphoreType.DMA((7,)),
         ],
         compiler_params=pltpu.CompilerParams(vmem_limit_bytes=42 * 2**20),
         cost_estimate=pl.CostEstimate(flops=20_000_000, bytes_accessed=2**20, transcendentals=0),
@@ -536,9 +559,16 @@
     plane = (1, rows_count, cols_count)
     smem = pl.BlockSpec(memory_space=pltpu.SMEM)
     vmem = pl.BlockSpec(memory_space=pltpu.VMEM)
-    low = pl.BlockSpec(plane, lambda i: (jnp.minimum(i, HALO - 1), 0, 0))
+
+    def low(which):
+        return pl.BlockSpec((None, *plane), lambda i: (which, jnp.minimum(i, HALO - 1), 0, 0))
+
+    def high(which):
+        return pl.BlockSpec(
+            (None, *plane), lambda i: (which, jnp.clip(i - HALO - own, 0, HALO - 1), 0, 0)
+        )
+
     middle = pl.BlockSpec(plane, lambda i: (jnp.clip(i - HALO, 0, own - 1), 0, 0))
-    high = pl.BlockSpec(plane, lambda i: (jnp.clip(i - HALO - own, 0, HALO - 1), 0, 0))
     columns_table = jnp.asarray(np.repeat(hartley(cols_count // R), R, axis=1))
     voxels = pl.BlockSpec(
         (1, rows_count, cols_count),
@@ -554,7 +584,7 @@
         sweep_kernel,
         grid=(total,),
         out_shape=jax.ShapeDtypeStruct((cols_count // R * (own // R), coarse), jnp.float32),
-        in_specs=[smem, low, middle, high, low, middle, high, vmem, vmem] + [voxels] * 4 + [vmem],
+        in_specs=[smem, low(0), middle, high(0), low(1), middle, high(1), vmem, vmem] + [voxels] * 4 + [vmem],
         out_specs=vmem,
         scratch_shapes=[padded(LONG)] * 2
         + [padded(SHORT)] * 3
@@ -663,8 +693,10 @@
     domain_count, tracer_count = lax.axis_size("domain"), lax.axis_size("tracer")
     full = slab * domain_count
     offset = lax.axis_index("domain") * slab
-    rate_low, rate_high = neighbours(log_rate[:HALO], log_rate[-HALO:])
-    state_low, state_high = neighbours(initial[0, :HALO], initial[0, -HALO:])
+    low, high = neighbours(
+        jnp.stack([log_rate[:HALO], initial[0, :HALO]]),
+        jnp.stack([log_rate[-HALO:], initial[0, -HALO:]]),
+    )
     keys, values, starts, rate_near, state_near = sort_probes(
         offset.astype(jnp.int32)[None],
         depth,
@@ -678,8 +710,8 @@
     )
     source_plane = (plane - (offset - HALO)) % full
     fields = bin_probes(starts, keys, values, rows_count, cols_count)
-    rates = (rate_low, rate_near, rate_high)
-    states = (state_low, state_near, state_high)
+    rates = (low, rate_near, high)
+    states = (low, state_near, high)
     spectral = sweep(source_plane, rates, states, velocity, profile, fields)
     first, planes, second = rows_count // R, slab // R, cols_count // R
     axes = ("domain", "tracer")

time: 115 us -> 113 us (0.983)
  starting transfers between devices: 21.5 us -> 14.4 us
  waiting for transfers between devices: 12.6 us -> 18.6 us
  local copies, waits for them, and re-layouts: 7.08 us -> 3.61 us
  other arithmetic: 0 us -> 2.96 us
    ppermute x2 -> x1, starting transfers between devices: 5.82 us -> 0.01 us  [neighbours(): lax.ppermute(first, 'domain', down)]
    ppermute x2 -> x1, waiting for transfers between devices: 0.01 us -> 4.17 us  [neighbours(): lax.ppermute(first, 'domain', down)]
    slice x1, local copies, waits for them, and re-layouts: 3.14 us -> 0.14 us  [local(): initial[0, :HALO]]
    another operation x0 -> x2, other arithmetic: none -> 2.96 us  [the longest x1 1.5 us: local(): jnp.stack([log_rate[:HALO], initial[0, :HALO]])]
    all_to_all x1, starting transfers between devices: 14 us -> 11.4 us  [local(): lax.all_to_all(spectral.reshape(second, planes, first), axes, split_axis=...]
    another operation x0 -> x1, local copies, waits for them, and re-layouts: none -> 1.83 us  [local(): jnp.stack([log_rate[:HALO], initial[0, :HALO]])]
    ppermute x2 -> x1, waiting for transfers between devices: 0.01 us -> 1.83 us  [neighbours(): lax.ppermute(last, 'domain', up)]
    squeeze x1 -> x0, local copies, waits for them, and re-layouts: 1.5 us -> none  [local(): state_low, state_high = neighbours(initial[0, :HALO], initial[0, -HALO:])]
  transfers between devices with their start and end apart: 5 -> 3, of which waited for: 1 -> 3; matrix products, arithmetic and copies ran while one was open for 2% -> 2% of each run, Pallas kernels for 17% -> 17%
where the time goes in v4:
time: 113 us; the launch traced here: 112 us
  Pallas kernels  58 us (51%)
  waiting for transfers between devices  18.6 us (16%)
  starting transfers between devices  14.4 us (13%)
  blocking collectives  13.9 us (12%)
  local copies, waits for them, and re-layouts  3.61 us (3%)
  other arithmetic  2.96 us (3%)
    pallas_call x1, Pallas kernels, sweep(): pl.pallas_call(sweep_kernel, grid=(total,), out_shape=jax.ShapeDtypeStruc...  36.2 us
    all_to_all x1, blocking collectives, local(): result = lax.all_to_all(back, axes, split_axis=0, concat_axis=0, tiled=True)  13.9 us
    all_to_all x1, waiting for transfers between devices, local(): lax.all_to_all(spectral.reshape(second, planes, first), axes, split_axis=...  12.6 us
    all_to_all x1, starting transfers between devices, local(): lax.all_to_all(spectral.reshape(second, planes, first), axes, split_axis=...  11.4 us
    pallas_call x1, Pallas kernels, sort_probes(): pl.pallas_call(sort_kernel, out_shape=(jax.ShapeDtypeStruct((shape[0] + 8...  9.98 us
    pallas_call x1, Pallas kernels, bin_probes(): pl.pallas_call(bin_kernel, grid=(places,), out_shape=(field,) * (2 * STEP...  9.21 us
    ppermute x1, waiting for transfers between devices, neighbours(): lax.ppermute(first, 'domain', down)  4.17 us
    ppermute x1, starting transfers between devices, neighbours(): lax.ppermute(last, 'domain', up)  3.03 us
  transfers between devices with their start and end apart: 3, of which 3 were waited for; matrix products, arithmetic and copies ran while one was open for 2% of the time, Pallas kernels for 17%

profile of v4, /device:TPU:1, one launch (start us, length us, event | category | flops | bytes accessed | tf_op | source)
XLA Modules:
  0.0 112.4 jit_solution(10187152146153572369)
XLA Ops:
  0.0 1.8 %slice_bitcast_fusion = (f32[1,4,256,256]{3,2,1,0:T(8,128)S(1)}, f32[1,4,256,256]{3,2,1,0:T(8,128)S(1)}) fusion(f32[16,256,256]{2,1,0:T(8,128)} %rate.1), kind=kLoop, calls=%fused_computation.2 | loop fusion | bytes 4194304 | tf_op jit(solution)/shard_map/stack | solution.py:697
  1.8 1.0 copy-done.11
  2.8 0.1 fusion
  3.0 0.0 copy-start.3
  3.0 0.0 copy-start.4
  3.0 0.0 copy-start.5
  3.0 0.0 copy-start.6
  3.0 0.0 copy-start.7
  3.0 1.5 %pad_maximum_fusion = f32[2,4,256,256]{3,2,1,0:T(8,128)} fusion(f32[1,4,256,256]{3,2,1,0:T(8,128)S(1)} %get-tuple-element.26, f32[1,4,256,256]{3,2,1,0:T(8,128)S(1)} %get-tuple-element.24), kind=kLoop, calls=%fused_computation | loop fusion | flops 524288 | bytes 4194304 | tf_op jit(solution)/shard_map/stack | solution.py:698
  4.5 3.0 %collective-permute-start = (f32[2,4,256,256]{3,2,1,0:T(8,128)}, f32[2,4,256,256]{3,2,1,0:T(8,128)S(1)}, u32[]{:S(2)}, u32[]{:S(2)}) collective-permute-start(f32[2,4,256,256]{3,2,1,0:T(8,128)} %pad_maximum_fusion), channel_id=1, source_target_pairs={{0,1},{1,2},{2,3},{3,4},{4,5},{5,6},{6,7},{7,8},{8,9},{9,10},{10,1... | collective-permute-start | bytes 6291464 | tf_op jit(solution)/shard_map/ppermute | solution.py:688
  7.5 1.5 %pad_maximum_fusion.1 = f32[2,4,256,256]{3,2,1,0:T(8,128)} fusion(f32[1,4,256,256]{3,2,1,0:T(8,128)S(1)} %get-tuple-element.25, f32[1,4,256,256]{3,2,1,0:T(8,128)S(1)} %get-tuple-element.23), kind=kLoop, calls=%fused_computation.1 | loop fusion | flops 524288 | bytes 4194304 | tf_op jit(solution)/shard_map/stack | solution.py:697
  9.0 0.0 collective-permute-start.1
  9.7 0.0 copy-done.3
  9.7 0.0 copy-start
  9.7 0.0 copy-start.1
  9.8 0.0 copy-start.8
  9.8 10.0 %sort_probes.1 = (s32[264,128]{1,0:T(8,128)S(1)}, f32[264,128]{1,0:T(8,128)S(1)}, s32[21]{0:T(128)S(1)}, f32[16,256,256]{2,1,0:T(8,128)S(1)}, f32[16,256,256]{2,1,0:T(8,128)S(1)}) custom-call(s32[1]{0:T(128)} %bitcast.2.offset_ref, s32[256,128]{1,0:T(8,128)S(1)} %bitcast.22, s32[256,128]{1,0:T(8,128)S(1)} %bitcast.23, s32[256,128]{1,0:T(8,128)S(1)} %bitcast.24, ...), custom_call_target="tpu_custom_call" | custom-call | flops 20000000 | bytes 1048576 | tf_op jit(solution)/shard_map/sort_probes/pallas_call | solution.py:210
  19.8 9.2 %bin_probes.1 = (f32[20,256,256]{2,1,0:T(8,128)S(1)}, f32[20,256,256]{2,1,0:T(8,128)S(1)}, f32[20,256,256]{2,1,0:T(8,128)S(1)}, f32[20,256,256]{2,1,0:T(8,128)S(1)}) custom-call(s32[21]{0:T(128)S(1)} %get-tuple-element.16.starts, s32[264,128]{1,0:T(8,128)S(1)} %get-tuple-element.17.keys_ref, f32[264,128]{1,0:T(8,128)S(1)} %get-tuple-element.18.values_ref), custom_call_target="tpu_custom_call" | custom-call | flops 30000000 | bytes 20971520 | tf_op jit(solution)/shard_map/bin_probes/pallas_call | solution.py:286
  29.0 1.8 %collective-permute-done.rate_low.state_low = f32[2,4,256,256]{3,2,1,0:T(8,128)S(1)} collective-permute-done((f32[2,4,256,256]{3,2,1,0:T(8,128)}, f32[2,4,256,256]{3,2,1,0:T(8,128)S(1)}, u32[]{:S(2)}, u32[]{:S(2)}) %collective-permute-start) | collective-permute-done | bytes 2097184 | tf_op jit(solution)/shard_map/ppermute | solution.py:688
  30.8 4.2 %collective-permute-done.1.rate_high.state_high = f32[2,4,256,256]{3,2,1,0:T(8,128)} collective-permute-done((f32[2,4,256,256]{3,2,1,0:T(8,128)}, f32[2,4,256,256]{3,2,1,0:T(8,128)}, u32[]{:S(2)}, u32[]{:S(2)}) %collective-permute-start.1) | collective-permute-done | bytes 2097184 | tf_op jit(solution)/shard_map/ppermute | solution.py:688
  35.0 0.0 copy-done.8
  35.0 0.0 copy-start.12
  35.0 0.0 copy-start.2
  35.0 0.0 copy-start.9
  35.0 0.0 copy-start.10
  35.0 36.2 %sweep.1 = f32[1024,128]{1,0:T(8,128)} custom-call(s32[1]{0:T(128)S(6)} %select_n.11.source_plane, f32[2,4,256,256]{3,2,1,0:T(8,128)S(1)} %collective-permute-done.rate_low.state_low, f32[16,256,256]{2,1,0:T(8,128)S(1)} %get-tuple-element.14.rate_own, f32[2,4,256,256]{3,2,1,0:T(8,128)} %collective-permute-done.1.rate_high.state_high, ...), custom_call_target="tpu_custom_call" | custom-call | flops 200000000 | bytes 35651584 | tf_op jit(solution)/shard_map/sweep/pallas_call | solution.py:583
  71.3 11.4 %all-to-all-start = ((f32[128,8,128]{2,1,0:T(8,128)}), f32[128,8,128]{2,1,0:T(8,128)S(1)}, u32[]{:S(2)}, u32[]{:S(2)}) async-start(f32[128,8,128]{2,1,0:T(8,128)} %bitcast.10), calls=%async_computation | async-start | bytes 1048576 | tf_op jit(solution)/shard_map/all_to_all | solution.py:718
  82.7 0.6 dynamic_slice.3.lam_second
  83.3 12.6 %all-to-all-done = f32[128,8,128]{2,1,0:T(8,128)S(1)} async-done(((f32[128,8,128]{2,1,0:T(8,128)}), f32[128,8,128]{2,1,0:T(8,128)S(1)}, u32[]{:S(2)}, u32[]{:S(2)}) %all-to-all-start) | async-done | bytes 524320 | tf_op jit(solution)/shard_map/all_to_all | solution.py:718
  95.8 1.7 %filter.1 = f32[128,128]{1,0:T(8,128)S(1)} custom-call(f32[1]{0:T(128)} %dynamic_slice.3.lam_second, f32[16,8,8,128]{3,2,1,0:T(8,128)S(1)} %bitcast.19, f32[128,128]{1,0:T(8,128)S(1)} %copy-done.2, f32[128,1]{1,0:T(8,128)S(1)} %copy-done.9, f32[1,128]{1,0:T(1,128)S(1)} %copy-done.10), custom_call_target="tpu_custom_call" | custom-call | tf_op jit(solution)/shard_map/filter/pallas_call | solution.py:645
  97.6 13.9 %all_to_all.16 = f32[128,1,128]{2,1,0:T(1,128)S(1)} all-to-all(f32[128,1,128]{2,1,0:T(1,128)S(1)} %bitcast.21), channel_id=1, replica_groups=mesh['tracer'=8,'domain'=16] {'domain','tracer'}, dimensions={0} | all-to-all | bytes 131072 | tf_op jit(solution)/shard_map/all_to_all | solution.py:724
  111.5 0.9 inverse_columns.1
  (11 shorter events, 0.0 us)
Async XLA Ops:
  0.0 2.8 %copy-start.11 = (f32[1,16,256,256]{3,2,1,0:T(8,128)S(1)}, f32[1,16,256,256]{3,2,1,0:T(8,128)}, u32[]{:S(2)}) copy-start(f32[1,16,256,256]{3,2,1,0:T(8,128)} %param.18) | copy-start | bytes 12582916
  3.0 6.7 %copy-start.3 = (s32[1,32768]{1,0:T(1,128)S(1)}, s32[1,32768]{1,0:T(1,128)}, u32[]{:S(2)}) copy-start(s32[1,32768]{1,0:T(1,128)} %param.21) | copy-start | bytes 393220
  3.0 6.7 %copy-start.4 = (s32[1,32768]{1,0:T(1,128)S(1)}, s32[1,32768]{1,0:T(1,128)}, u32[]{:S(2)}) copy-start(s32[1,32768]{1,0:T(1,128)} %param.22) | copy-start | bytes 393220
  3.0 6.7 %copy-start.5 = (s32[1,32768]{1,0:T(1,128)S(1)}, s32[1,32768]{1,0:T(1,128)}, u32[]{:S(2)}) copy-start(s32[1,32768]{1,0:T(1,128)} %param.23) | copy-start | bytes 393220
  3.0 6.7 %copy-start.6 = (s32[1,32768]{1,0:T(1,128)S(1)}, s32[1,32768]{1,0:T(1,128)}, u32[]{:S(2)}) copy-start(s32[1,32768]{1,0:T(1,128)} %param.24) | copy-start | bytes 393220
  3.0 6.7 %copy-start.7 = (f32[1,32768]{1,0:T(1,128)S(1)}, f32[1,32768]{1,0:T(1,128)}, u32[]{:S(2)}) copy-start(f32[1,32768]{1,0:T(1,128)} %param.25) | copy-start | bytes 393220
  4.5 26.3 %collective-permute-start = (f32[2,4,256,256]{3,2,1,0:T(8,128)}, f32[2,4,256,256]{3,2,1,0:T(8,128)S(1)}, u32[]{:S(2)}, u32[]{:S(2)}) collective-permute-start(f32[2,4,256,256]{3,2,1,0:T(8,128)} %pad_maximum_fusion), channel_id=1, source_target_pairs={{0,1},{1,2},{2,3},{3,4},{4,5},{5,6},{6,7},{7,8},{8,9},{9,10},{10,1... | collective-permute-start | bytes 6291464 | tf_op jit(solution)/shard_map/ppermute | solution.py:688
  9.0 26.0 %collective-permute-start.1 = (f32[2,4,256,256]{3,2,1,0:T(8,128)}, f32[2,4,256,256]{3,2,1,0:T(8,128)}, u32[]{:S(2)}, u32[]{:S(2)}) collective-permute-start(f32[2,4,256,256]{3,2,1,0:T(8,128)} %pad_maximum_fusion.1), channel_id=1, source_target_pairs={{1,0},{2,1},{3,2},{4,3},{5,4},{6,5},{7,6},{8,7},{9,8},{10,9},{11,1... | collective-permute-start | bytes 6291464 | tf_op jit(solution)/shard_map/ppermute | solution.py:688
  9.7 25.2 %copy-start = (f32[256,256]{1,0:T(8,128)S(1)}, f32[256,256]{1,0:T(8,128)}, u32[]{:S(2)}) copy-start(f32[256,256]{1,0:T(8,128)} %velocity_ref.1) | copy-start | bytes 786436
  9.7 25.2 %copy-start.1 = (f32[1,256,256]{2,1,0:T(8,128)S(1)}, f32[1,256,256]{2,1,0:T(8,128)}, u32[]{:S(2)}) copy-start(f32[1,256,256]{2,1,0:T(8,128)} %profile_ref.1) | copy-start | bytes 786436
  9.8 25.2 %copy-start.8 = (f32[128,256]{1,0:T(8,128)S(1)}, f32[128,256]{1,0:T(8,128)}, u32[]{:S(2)}) copy-start(f32[128,256]{1,0:T(8,128)} %constant.49.clone.columns_table) | copy-start | bytes 393220
  35.0 47.7 %copy-start.12 = (f32[128]{0:T(128)S(1)}, f32[128]{0:T(128)}, u32[]{:S(2)}) copy-start(f32[128]{0:T(128)} %constant.50.clone) | copy-start | bytes 1540
  35.0 60.8 %copy-start.2 = (f32[128,128]{1,0:T(8,128)S(1)}, f32[128,128]{1,0:T(8,128)}, u32[]{:S(2)}) copy-start(f32[128,128]{1,0:T(8,128)} %constant.51.clone.table_ref) | copy-start | bytes 196612
  35.0 60.8 %copy-start.9 = (f32[128,1]{1,0:T(8,128)S(1)}, f32[128,1]{1,0:T(8,128)}, u32[]{:S(2)}) copy-start(f32[128,1]{1,0:T(8,128)} %constant.52.clone.symbol_depth) | copy-start | bytes 1540
  35.0 60.8 %copy-start.10 = (f32[1,128]{1,0:T(1,128)S(1)}, f32[1,128]{1,0:T(1,128)}, u32[]{:S(2)}) copy-start(f32[1,128]{1,0:T(1,128)} %constant.53.clone.symbol_rows) | copy-start | bytes 1540
  71.3 24.6 %all-to-all-start = ((f32[128,8,128]{2,1,0:T(8,128)}), f32[128,8,128]{2,1,0:T(8,128)S(1)}, u32[]{:S(2)}, u32[]{:S(2)}) async-start(f32[128,8,128]{2,1,0:T(8,128)} %bitcast.10), calls=%async_computation | async-start | bytes 1048576 | tf_op jit(solution)/shard_map/all_to_all | solution.py:718

commit v5 on v4

--- a/solution.py
+++ b/solution.py
@@ -681,6 +681,34 @@
     )(received, jnp.asarray(hartley(received.shape[0])))
 
 
+def edges_kernel(rate, state, first, last, sems):
+    begin = rate.shape[0] - HALO
+    copies = [
+        pltpu.make_async_copy(source.at[pl.ds(at, HALO)], target.at[which], sems.at[which, side])
+        for which, source in enumerate((rate, state))
+        for side, (at, target) in enumerate(((0, first), (begin, last)))
+    ]
+    for copy in copies:
+        copy.start()
+    for copy in copies:
+        copy.wait()
+
+
+def edges(rate, state):
+    stay = pl.BlockSpec(memory_space=pl.ANY)
+    vmem = pl.BlockSpec(memory_space=pltpu.VMEM)
+    end = jax.ShapeDtypeStruct((2, HALO, *rate.shape[1:]), jnp.float32)
+    return pl.pallas_call(
+        edges_kernel,
+        out_shape=(end, end),
+        in_specs=[stay, stay],
+        out_specs=(vmem, vmem),
+        scratch_shapes=[pltpu.SemaphoreType.DMA((2, 2))],
+        compiler_params=pltpu.CompilerParams(vmem_limit_bytes=50 * 2**20),
+        name="edges",
+    )(rate, state)
+
+
 def neighbours(first, last):
     count = lax.axis_size("domain")
     up = [(i, (i + 1) % count) for i in range(count)]
@@ -693,10 +721,7 @@
     domain_count, tracer_count = lax.axis_size("domain"), lax.axis_size("tracer")
     full = slab * domain_count
     offset = lax.axis_index("domain") * slab
-    low, high = neighbours(
-        jnp.stack([log_rate[:HALO], initial[0, :HALO]]),
-        jnp.stack([log_rate[-HALO:], initial[0, -HALO:]]),
-    )
+    low, high = neighbours(*edges(log_rate, initial[0]))
     keys, values, starts, rate_near, state_near = sort_probes(
         offset.astype(jnp.int32)[None],
         depth,

time: 113 us -> 111 us (0.982)
  Pallas kernels: 58 us -> 64.4 us
  other arithmetic: 2.96 us -> 0 us
  local copies, waits for them, and re-layouts: 3.61 us -> 0.65 us
  waiting for transfers between devices: 18.6 us -> 16.5 us
    pallas_call x0 -> x1, Pallas kernels: none -> 4.31 us  [edges(): pl.pallas_call(edges_kernel, out_shape=(end, end), in_specs=[stay, stay],...]
    another operation x2 -> x0, other arithmetic: 2.96 us -> none  [the longest x1 1.5 us: local(): jnp.stack([log_rate[:HALO], initial[0, :HALO]])]
    pallas_call x1, Pallas kernels: 9.21 us -> 11.3 us  [bin_probes(): pl.pallas_call(bin_kernel, grid=(places,), out_shape=(field,) * (2 * STEP...]
    another operation x1 -> x0, local copies, waits for them, and re-layouts: 1.83 us -> none  [local(): jnp.stack([log_rate[:HALO], initial[0, :HALO]])]
    ppermute x1, waiting for transfers between devices: 4.17 us -> 2.67 us  [neighbours(): lax.ppermute(first, 'domain', down)]
  transfers between devices with their start and end apart: 3 -> 3, of which waited for: 3 -> 3; matrix products, arithmetic and copies ran while one was open for 2% -> 1% of each run, Pallas kernels for 17% -> 19%
where the time goes in v5:
time: 111 us
  Pallas kernels  64.4 us (58%)
  waiting for transfers between devices  16.5 us (15%)
  starting transfers between devices  14.5 us (13%)
  blocking collectives  13.9 us (13%)
    pallas_call x1, Pallas kernels, sweep(): pl.pallas_call(sweep_kernel, grid=(total,), out_shape=jax.ShapeDtypeStruc...  36.2 us
    all_to_all x1, blocking collectives, local(): result = lax.all_to_all(back, axes, split_axis=0, concat_axis=0, tiled=True)  13.9 us
    all_to_all x1, waiting for transfers between devices, local(): lax.all_to_all(spectral.reshape(second, planes, first), axes, split_axis=...  12.6 us
    all_to_all x1, starting transfers between devices, local(): lax.all_to_all(spectral.reshape(second, planes, first), axes, split_axis=...  11.4 us
    pallas_call x1, Pallas kernels, bin_probes(): pl.pallas_call(bin_kernel, grid=(places,), out_shape=(field,) * (2 * STEP...  11.3 us
    pallas_call x1, Pallas kernels, sort_probes(): pl.pallas_call(sort_kernel, out_shape=(jax.ShapeDtypeStruct((shape[0] + 8...  9.98 us
    pallas_call x1, Pallas kernels, edges(): pl.pallas_call(edges_kernel, out_shape=(end, end), in_specs=[stay, stay],...  4.31 us
    ppermute x1, starting transfers between devices, neighbours(): lax.ppermute(last, 'domain', up)  3.1 us
  transfers between devices with their start and end apart: 3, of which 3 were waited for; matrix products, arithmetic and copies ran while one was open for 1% of the time, Pallas kernels for 19%

profile of v5, /device:TPU:1, one launch (start us, length us, event | category | flops | bytes accessed | tf_op | source)
XLA Modules:
  0.0 110.8 jit_solution(1705726346186371240)
XLA Ops:
  0.0 0.0 copy-start.6
  0.0 0.0 copy-start.7
  0.0 4.3 %edges.1 = (f32[2,4,256,256]{3,2,1,0:T(8,128)}, f32[2,4,256,256]{3,2,1,0:T(8,128)}) custom-call(f32[16,256,256]{2,1,0:T(8,128)} %rate.3, f32[16,256,256]{2,1,0:T(8,128)} %bitcast.23), custom_call_target="tpu_custom_call" | custom-call | tf_op jit(solution)/shard_map/edges/pallas_call | solution.py:701
  4.3 3.1 %collective-permute-start = (f32[2,4,256,256]{3,2,1,0:T(8,128)}, f32[2,4,256,256]{3,2,1,0:T(8,128)S(1)}, u32[]{:S(2)}, u32[]{:S(2)}) collective-permute-start(f32[2,4,256,256]{3,2,1,0:T(8,128)} %get-tuple-element.16), channel_id=1, source_target_pairs={{0,1},{1,2},{2,3},{3,4},{4,5},{5,6},{6,7},{7,8},{8,9},{9,10},{10,1... | collective-permute-start | bytes 6291464 | tf_op jit(solution)/shard_map/ppermute | solution.py:716
  7.4 0.0 collective-permute-start.1
  8.1 0.0 copy-done.3
  8.1 0.0 copy-done.4
  8.1 0.0 copy-done.5
  8.1 0.0 copy-done.6
  8.2 0.0 copy-done.7
  8.2 0.0 copy-start
  8.2 0.0 copy-start.1
  8.2 0.0 copy-start.8
  8.2 10.0 %sort_probes.1 = (s32[264,128]{1,0:T(8,128)S(1)}, f32[264,128]{1,0:T(8,128)S(1)}, s32[21]{0:T(128)S(1)}, f32[16,256,256]{2,1,0:T(8,128)S(1)}, f32[16,256,256]{2,1,0:T(8,128)S(1)}) custom-call(s32[1]{0:T(128)} %bitcast.2.offset_ref, s32[256,128]{1,0:T(8,128)S(1)} %bitcast.18, s32[256,128]{1,0:T(8,128)S(1)} %bitcast.19, s32[256,128]{1,0:T(8,128)S(1)} %bitcast.20, ...), custom_call_target="tpu_custom_call" | custom-call | flops 20000000 | bytes 1048576 | tf_op jit(solution)/shard_map/sort_probes/pallas_call | solution.py:210
  18.2 11.3 %bin_probes.1 = (f32[20,256,256]{2,1,0:T(8,128)S(1)}, f32[20,256,256]{2,1,0:T(8,128)S(1)}, f32[20,256,256]{2,1,0:T(8,128)S(1)}, f32[20,256,256]{2,1,0:T(8,128)S(1)}) custom-call(s32[21]{0:T(128)S(1)} %get-tuple-element.20.starts, s32[264,128]{1,0:T(8,128)S(1)} %get-tuple-element.21.keys_ref, f32[264,128]{1,0:T(8,128)S(1)} %get-tuple-element.22.values_ref), custom_call_target="tpu_custom_call" | custom-call | flops 30000000 | bytes 20971520 | tf_op jit(solution)/shard_map/bin_probes/pallas_call | solution.py:286
  29.5 1.2 %collective-permute-done.rate_low.state_low = f32[2,4,256,256]{3,2,1,0:T(8,128)S(1)} collective-permute-done((f32[2,4,256,256]{3,2,1,0:T(8,128)}, f32[2,4,256,256]{3,2,1,0:T(8,128)S(1)}, u32[]{:S(2)}, u32[]{:S(2)}) %collective-permute-start) | collective-permute-done | bytes 2097184 | tf_op jit(solution)/shard_map/ppermute | solution.py:716
  30.7 2.7 %collective-permute-done.1.rate_high.state_high = f32[2,4,256,256]{3,2,1,0:T(8,128)} collective-permute-done((f32[2,4,256,256]{3,2,1,0:T(8,128)}, f32[2,4,256,256]{3,2,1,0:T(8,128)}, u32[]{:S(2)}, u32[]{:S(2)}) %collective-permute-start.1) | collective-permute-done | bytes 2097184 | tf_op jit(solution)/shard_map/ppermute | solution.py:716
  33.4 0.0 copy-done.8
  33.4 0.0 copy-start.11
  33.4 0.0 copy-start.2
  33.4 0.0 copy-start.9
  33.5 0.0 copy-start.10
  33.5 36.2 %sweep.1 = f32[1024,128]{1,0:T(8,128)} custom-call(s32[1]{0:T(128)S(6)} %select_n.11.source_plane, f32[2,4,256,256]{3,2,1,0:T(8,128)S(1)} %collective-permute-done.rate_low.state_low, f32[16,256,256]{2,1,0:T(8,128)S(1)} %get-tuple-element.17.rate_own, f32[2,4,256,256]{3,2,1,0:T(8,128)} %collective-permute-done.1.rate_high.state_high, ...), custom_call_target="tpu_custom_call" | custom-call | flops 200000000 | bytes 35651584 | tf_op jit(solution)/shard_map/sweep/pallas_call | solution.py:583
  69.7 11.4 %all-to-all-start = ((f32[128,8,128]{2,1,0:T(8,128)}), f32[128,8,128]{2,1,0:T(8,128)S(1)}, u32[]{:S(2)}, u32[]{:S(2)}) async-start(f32[128,8,128]{2,1,0:T(8,128)} %bitcast.8), calls=%async_computation | async-start | bytes 1048576 | tf_op jit(solution)/shard_map/all_to_all | solution.py:743
  81.1 0.0 copy-done.11
  81.1 0.6 dynamic_slice.3.lam_second
  81.7 12.6 %all-to-all-done = f32[128,8,128]{2,1,0:T(8,128)S(1)} async-done(((f32[128,8,128]{2,1,0:T(8,128)}), f32[128,8,128]{2,1,0:T(8,128)S(1)}, u32[]{:S(2)}, u32[]{:S(2)}) %all-to-all-start) | async-done | bytes 524320 | tf_op jit(solution)/shard_map/all_to_all | solution.py:743
  94.3 0.0 copy-done.2
  94.3 0.0 copy-done.10
  94.3 1.7 %filter.1 = f32[128,128]{1,0:T(8,128)S(1)} custom-call(f32[1]{0:T(128)} %dynamic_slice.3.lam_second, f32[16,8,8,128]{3,2,1,0:T(8,128)S(1)} %bitcast.15, f32[128,128]{1,0:T(8,128)S(1)} %copy-done.2, f32[128,1]{1,0:T(8,128)S(1)} %copy-done.9, f32[1,128]{1,0:T(1,128)S(1)} %copy-done.10), custom_call_target="tpu_custom_call" | custom-call | tf_op jit(solution)/shard_map/filter/pallas_call | solution.py:645
  96.0 13.9 %all_to_all.16 = f32[128,1,128]{2,1,0:T(1,128)S(1)} all-to-all(f32[128,1,128]{2,1,0:T(1,128)S(1)} %bitcast.17), channel_id=1, replica_groups=mesh['tracer'=8,'domain'=16] {'domain','tracer'}, dimensions={0} | all-to-all | bytes 131072 | tf_op jit(solution)/shard_map/all_to_all | solution.py:749
  109.9 0.9 inverse_columns.1
  (6 shorter events, 0.0 us)
Async XLA Ops:
  0.0 8.1 %copy-start.3 = (s32[1,32768]{1,0:T(1,128)S(1)}, s32[1,32768]{1,0:T(1,128)}, u32[]{:S(2)}) copy-start(s32[1,32768]{1,0:T(1,128)} %param.21) | copy-start | bytes 393220
  0.0 8.1 %copy-start.4 = (s32[1,32768]{1,0:T(1,128)S(1)}, s32[1,32768]{1,0:T(1,128)}, u32[]{:S(2)}) copy-start(s32[1,32768]{1,0:T(1,128)} %param.22) | copy-start | bytes 393220
  0.0 8.1 %copy-start.5 = (s32[1,32768]{1,0:T(1,128)S(1)}, s32[1,32768]{1,0:T(1,128)}, u32[]{:S(2)}) copy-start(s32[1,32768]{1,0:T(1,128)} %param.23) | copy-start | bytes 393220
  0.0 8.1 %copy-start.6 = (s32[1,32768]{1,0:T(1,128)S(1)}, s32[1,32768]{1,0:T(1,128)}, u32[]{:S(2)}) copy-start(s32[1,32768]{1,0:T(1,128)} %param.24) | copy-start | bytes 393220
  0.0 8.1 %copy-start.7 = (f32[1,32768]{1,0:T(1,128)S(1)}, f32[1,32768]{1,0:T(1,128)}, u32[]{:S(2)}) copy-start(f32[1,32768]{1,0:T(1,128)} %param.25) | copy-start | bytes 393220
  4.3 26.4 %collective-permute-start = (f32[2,4,256,256]{3,2,1,0:T(8,128)}, f32[2,4,256,256]{3,2,1,0:T(8,128)S(1)}, u32[]{:S(2)}, u32[]{:S(2)}) collective-permute-start(f32[2,4,256,256]{3,2,1,0:T(8,128)} %get-tuple-element.16), channel_id=1, source_target_pairs={{0,1},{1,2},{2,3},{3,4},{4,5},{5,6},{6,7},{7,8},{8,9},{9,10},{10,1... | collective-permute-start | bytes 6291464 | tf_op jit(solution)/shard_map/ppermute | solution.py:716
  7.4 26.0 %collective-permute-start.1 = (f32[2,4,256,256]{3,2,1,0:T(8,128)}, f32[2,4,256,256]{3,2,1,0:T(8,128)}, u32[]{:S(2)}, u32[]{:S(2)}) collective-permute-start(f32[2,4,256,256]{3,2,1,0:T(8,128)} %get-tuple-element.18), channel_id=1, source_target_pairs={{1,0},{2,1},{3,2},{4,3},{5,4},{6,5},{7,6},{8,7},{9,8},{10,9},{11,1... | collective-permute-start | bytes 6291464 | tf_op jit(solution)/shard_map/ppermute | solution.py:716
  8.2 25.2 %copy-start = (f32[256,256]{1,0:T(8,128)S(1)}, f32[256,256]{1,0:T(8,128)}, u32[]{:S(2)}) copy-start(f32[256,256]{1,0:T(8,128)} %velocity_ref.1) | copy-start | bytes 786436
  8.2 25.2 %copy-start.1 = (f32[1,256,256]{2,1,0:T(8,128)S(1)}, f32[1,256,256]{2,1,0:T(8,128)}, u32[]{:S(2)}) copy-start(f32[1,256,256]{2,1,0:T(8,128)} %profile_ref.1) | copy-start | bytes 786436
  8.2 25.2 %copy-start.8 = (f32[128,256]{1,0:T(8,128)S(1)}, f32[128,256]{1,0:T(8,128)}, u32[]{:S(2)}) copy-start(f32[128,256]{1,0:T(8,128)} %constant.49.clone.columns_table) | copy-start | bytes 393220
  33.4 47.7 %copy-start.11 = (f32[128]{0:T(128)S(1)}, f32[128]{0:T(128)}, u32[]{:S(2)}) copy-start(f32[128]{0:T(128)} %constant.50.clone) | copy-start | bytes 1540
  33.4 60.9 %copy-start.2 = (f32[128,128]{1,0:T(8,128)S(1)}, f32[128,128]{1,0:T(8,128)}, u32[]{:S(2)}) copy-start(f32[128,128]{1,0:T(8,128)} %constant.51.clone.table_ref) | copy-start | bytes 196612
  33.4 60.9 %copy-start.9 = (f32[128,1]{1,0:T(8,128)S(1)}, f32[128,1]{1,0:T(8,128)}, u32[]{:S(2)}) copy-start(f32[128,1]{1,0:T(8,128)} %constant.52.clone.symbol_depth) | copy-start | bytes 1540
  33.5 60.8 %copy-start.10 = (f32[1,128]{1,0:T(1,128)S(1)}, f32[1,128]{1,0:T(1,128)}, u32[]{:S(2)}) copy-start(f32[1,128]{1,0:T(1,128)} %constant.53.clone.symbol_rows) | copy-start | bytes 1540
  69.7 24.6 %all-to-all-start = ((f32[128,8,128]{2,1,0:T(8,128)}), f32[128,8,128]{2,1,0:T(8,128)S(1)}, u32[]{:S(2)}, u32[]{:S(2)}) async-start(f32[128,8,128]{2,1,0:T(8,128)} %bitcast.8), calls=%async_computation | async-start | bytes 1048576 | tf_op jit(solution)/shard_map/all_to_all | solution.py:743

commit v6 on v5

--- a/solution.py
+++ b/solution.py
@@ -704,7 +704,7 @@
         in_specs=[stay, stay],
         out_specs=(vmem, vmem),
         scratch_shapes=[pltpu.SemaphoreType.DMA((2, 2))],
-        compiler_params=pltpu.CompilerParams(vmem_limit_bytes=50 * 2**20),
+        compiler_params=pltpu.CompilerParams(vmem_limit_bytes=47 * 2**20),
         name="edges",
     )(rate, state)
 

time: 111 us -> 111 us (level)
  Pallas kernels: 64.4 us -> 62.3 us
  waiting for transfers between devices: 16.5 us -> 18.6 us
    ppermute x1, waiting for transfers between devices: 1.24 us -> 3.33 us  [neighbours(): lax.ppermute(last, 'domain', up)]
    pallas_call x1, Pallas kernels: 11.3 us -> 9.21 us  [bin_probes(): pl.pallas_call(bin_kernel, grid=(places,), out_shape=(field,) * (2 * STEP...]
  transfers between devices with their start and end apart: 3 -> 3, of which waited for: 3 -> 3; matrix products, arithmetic and copies ran while one was open for 1% -> 1% of each run, Pallas kernels for 19% -> 17%
where the time goes in v6:
time: 111 us
  Pallas kernels  62.3 us (56%)
  waiting for transfers between devices  18.6 us (17%)
  starting transfers between devices  14.5 us (13%)
  blocking collectives  13.9 us (13%)
    pallas_call x1, Pallas kernels, sweep(): pl.pallas_call(sweep_kernel, grid=(total,), out_shape=jax.ShapeDtypeStruc...  36.2 us
    all_to_all x1, blocking collectives, local(): result = lax.all_to_all(back, axes, split_axis=0, concat_axis=0, tiled=True)  13.9 us
    all_to_all x1, waiting for transfers between devices, local(): lax.all_to_all(spectral.reshape(second, planes, first), axes, split_axis=...  12.6 us
    all_to_all x1, starting transfers between devices, local(): lax.all_to_all(spectral.reshape(second, planes, first), axes, split_axis=...  11.4 us
    pallas_call x1, Pallas kernels, sort_probes(): pl.pallas_call(sort_kernel, out_shape=(jax.ShapeDtypeStruct((shape[0] + 8...  9.98 us
    pallas_call x1, Pallas kernels, bin_probes(): pl.pallas_call(bin_kernel, grid=(places,), out_shape=(field,) * (2 * STEP...  9.21 us
    pallas_call x1, Pallas kernels, edges(): pl.pallas_call(edges_kernel, out_shape=(end, end), in_specs=[stay, stay],...  4.31 us
    ppermute x1, waiting for transfers between devices, neighbours(): lax.ppermute(last, 'domain', up)  3.33 us
  transfers between devices with their start and end apart: 3, of which 3 were waited for; matrix products, arithmetic and copies ran while one was open for 1% of the time, Pallas kernels for 17%

profile of v6, /device:TPU:1, one launch (start us, length us, event | category | flops | bytes accessed | tf_op | source)
XLA Modules:
  0.0 110.8 jit_solution(1705726346186371240)
XLA Ops:
  0.0 0.0 copy-start.6
  0.0 0.0 copy-start.7
  0.0 4.3 %edges.1 = (f32[2,4,256,256]{3,2,1,0:T(8,128)}, f32[2,4,256,256]{3,2,1,0:T(8,128)}) custom-call(f32[16,256,256]{2,1,0:T(8,128)} %rate.3, f32[16,256,256]{2,1,0:T(8,128)} %bitcast.23), custom_call_target="tpu_custom_call" | custom-call | tf_op jit(solution)/shard_map/edges/pallas_call | solution.py:701
  4.3 3.1 %collective-permute-start = (f32[2,4,256,256]{3,2,1,0:T(8,128)}, f32[2,4,256,256]{3,2,1,0:T(8,128)S(1)}, u32[]{:S(2)}, u32[]{:S(2)}) collective-permute-start(f32[2,4,256,256]{3,2,1,0:T(8,128)} %get-tuple-element.16), channel_id=1, source_target_pairs={{0,1},{1,2},{2,3},{3,4},{4,5},{5,6},{6,7},{7,8},{8,9},{9,10},{10,1... | collective-permute-start | bytes 6291464 | tf_op jit(solution)/shard_map/ppermute | solution.py:716
  7.4 0.0 collective-permute-start.1
  8.1 0.0 copy-done.3
  8.1 0.0 copy-done.4
  8.1 0.0 copy-done.5
  8.1 0.0 copy-done.6
  8.2 0.0 copy-done.7
  8.2 0.0 copy-start
  8.2 0.0 copy-start.1
  8.2 0.0 copy-start.8
  8.2 10.0 %sort_probes.1 = (s32[264,128]{1,0:T(8,128)S(1)}, f32[264,128]{1,0:T(8,128)S(1)}, s32[21]{0:T(128)S(1)}, f32[16,256,256]{2,1,0:T(8,128)S(1)}, f32[16,256,256]{2,1,0:T(8,128)S(1)}) custom-call(s32[1]{0:T(128)} %bitcast.2.offset_ref, s32[256,128]{1,0:T(8,128)S(1)} %bitcast.18, s32[256,128]{1,0:T(8,128)S(1)} %bitcast.19, s32[256,128]{1,0:T(8,128)S(1)} %bitcast.20, ...), custom_call_target="tpu_custom_call" | custom-call | flops 20000000 | bytes 1048576 | tf_op jit(solution)/shard_map/sort_probes/pallas_call | solution.py:210
  18.2 9.2 %bin_probes.1 = (f32[20,256,256]{2,1,0:T(8,128)S(1)}, f32[20,256,256]{2,1,0:T(8,128)S(1)}, f32[20,256,256]{2,1,0:T(8,128)S(1)}, f32[20,256,256]{2,1,0:T(8,128)S(1)}) custom-call(s32[21]{0:T(128)S(1)} %get-tuple-element.20.starts, s32[264,128]{1,0:T(8,128)S(1)} %get-tuple-element.21.keys_ref, f32[264,128]{1,0:T(8,128)S(1)} %get-tuple-element.22.values_ref), custom_call_target="tpu_custom_call" | custom-call | flops 30000000 | bytes 20971520 | tf_op jit(solution)/shard_map/bin_probes/pallas_call | solution.py:286
  27.4 3.3 %collective-permute-done.rate_low.state_low = f32[2,4,256,256]{3,2,1,0:T(8,128)S(1)} collective-permute-done((f32[2,4,256,256]{3,2,1,0:T(8,128)}, f32[2,4,256,256]{3,2,1,0:T(8,128)S(1)}, u32[]{:S(2)}, u32[]{:S(2)}) %collective-permute-start) | collective-permute-done | bytes 2097184 | tf_op jit(solution)/shard_map/ppermute | solution.py:716
  30.7 2.7 %collective-permute-done.1.rate_high.state_high = f32[2,4,256,256]{3,2,1,0:T(8,128)} collective-permute-done((f32[2,4,256,256]{3,2,1,0:T(8,128)}, f32[2,4,256,256]{3,2,1,0:T(8,128)}, u32[]{:S(2)}, u32[]{:S(2)}) %collective-permute-start.1) | collective-permute-done | bytes 2097184 | tf_op jit(solution)/shard_map/ppermute | solution.py:716
  33.4 0.0 copy-done.8
  33.4 0.0 copy-start.11
  33.4 0.0 copy-start.2
  33.4 0.0 copy-start.9
  33.5 0.0 copy-start.10
  33.5 36.2 %sweep.1 = f32[1024,128]{1,0:T(8,128)} custom-call(s32[1]{0:T(128)S(6)} %select_n.11.source_plane, f32[2,4,256,256]{3,2,1,0:T(8,128)S(1)} %collective-permute-done.rate_low.state_low, f32[16,256,256]{2,1,0:T(8,128)S(1)} %get-tuple-element.17.rate_own, f32[2,4,256,256]{3,2,1,0:T(8,128)} %collective-permute-done.1.rate_high.state_high, ...), custom_call_target="tpu_custom_call" | custom-call | flops 200000000 | bytes 35651584 | tf_op jit(solution)/shard_map/sweep/pallas_call | solution.py:583
  69.7 11.4 %all-to-all-start = ((f32[128,8,128]{2,1,0:T(8,128)}), f32[128,8,128]{2,1,0:T(8,128)S(1)}, u32[]{:S(2)}, u32[]{:S(2)}) async-start(f32[128,8,128]{2,1,0:T(8,128)} %bitcast.8), calls=%async_computation | async-start | bytes 1048576 | tf_op jit(solution)/shard_map/all_to_all | solution.py:743
  81.1 0.0 copy-done.11
  81.1 0.6 dynamic_slice.3.lam_second
  81.7 12.6 %all-to-all-done = f32[128,8,128]{2,1,0:T(8,128)S(1)} async-done(((f32[128,8,128]{2,1,0:T(8,128)}), f32[128,8,128]{2,1,0:T(8,128)S(1)}, u32[]{:S(2)}, u32[]{:S(2)}) %all-to-all-start) | async-done | bytes 524320 | tf_op jit(solution)/shard_map/all_to_all | solution.py:743
  94.3 0.0 copy-done.2
  94.3 0.0 copy-done.10
  94.3 1.7 %filter.1 = f32[128,128]{1,0:T(8,128)S(1)} custom-call(f32[1]{0:T(128)} %dynamic_slice.3.lam_second, f32[16,8,8,128]{3,2,1,0:T(8,128)S(1)} %bitcast.15, f32[128,128]{1,0:T(8,128)S(1)} %copy-done.2, f32[128,1]{1,0:T(8,128)S(1)} %copy-done.9, f32[1,128]{1,0:T(1,128)S(1)} %copy-done.10), custom_call_target="tpu_custom_call" | custom-call | tf_op jit(solution)/shard_map/filter/pallas_call | solution.py:645
  96.0 13.9 %all_to_all.16 = f32[128,1,128]{2,1,0:T(1,128)S(1)} all-to-all(f32[128,1,128]{2,1,0:T(1,128)S(1)} %bitcast.17), channel_id=1, replica_groups=mesh['tracer'=8,'domain'=16] {'domain','tracer'}, dimensions={0} | all-to-all | bytes 131072 | tf_op jit(solution)/shard_map/all_to_all | solution.py:749
  109.9 0.9 inverse_columns.1
  (6 shorter events, 0.0 us)
Async XLA Ops:
  0.0 8.1 %copy-start.3 = (s32[1,32768]{1,0:T(1,128)S(1)}, s32[1,32768]{1,0:T(1,128)}, u32[]{:S(2)}) copy-start(s32[1,32768]{1,0:T(1,128)} %param.21) | copy-start | bytes 393220
  0.0 8.1 %copy-start.4 = (s32[1,32768]{1,0:T(1,128)S(1)}, s32[1,32768]{1,0:T(1,128)}, u32[]{:S(2)}) copy-start(s32[1,32768]{1,0:T(1,128)} %param.22) | copy-start | bytes 393220
  0.0 8.1 %copy-start.5 = (s32[1,32768]{1,0:T(1,128)S(1)}, s32[1,32768]{1,0:T(1,128)}, u32[]{:S(2)}) copy-start(s32[1,32768]{1,0:T(1,128)} %param.23) | copy-start | bytes 393220
  0.0 8.1 %copy-start.6 = (s32[1,32768]{1,0:T(1,128)S(1)}, s32[1,32768]{1,0:T(1,128)}, u32[]{:S(2)}) copy-start(s32[1,32768]{1,0:T(1,128)} %param.24) | copy-start | bytes 393220
  0.0 8.1 %copy-start.7 = (f32[1,32768]{1,0:T(1,128)S(1)}, f32[1,32768]{1,0:T(1,128)}, u32[]{:S(2)}) copy-start(f32[1,32768]{1,0:T(1,128)} %param.25) | copy-start | bytes 393220
  4.3 26.4 %collective-permute-start = (f32[2,4,256,256]{3,2,1,0:T(8,128)}, f32[2,4,256,256]{3,2,1,0:T(8,128)S(1)}, u32[]{:S(2)}, u32[]{:S(2)}) collective-permute-start(f32[2,4,256,256]{3,2,1,0:T(8,128)} %get-tuple-element.16), channel_id=1, source_target_pairs={{0,1},{1,2},{2,3},{3,4},{4,5},{5,6},{6,7},{7,8},{8,9},{9,10},{10,1... | collective-permute-start | bytes 6291464 | tf_op jit(solution)/shard_map/ppermute | solution.py:716
  7.4 26.0 %collective-permute-start.1 = (f32[2,4,256,256]{3,2,1,0:T(8,128)}, f32[2,4,256,256]{3,2,1,0:T(8,128)}, u32[]{:S(2)}, u32[]{:S(2)}) collective-permute-start(f32[2,4,256,256]{3,2,1,0:T(8,128)} %get-tuple-element.18), channel_id=1, source_target_pairs={{1,0},{2,1},{3,2},{4,3},{5,4},{6,5},{7,6},{8,7},{9,8},{10,9},{11,1... | collective-permute-start | bytes 6291464 | tf_op jit(solution)/shard_map/ppermute | solution.py:716
  8.2 25.2 %copy-start = (f32[256,256]{1,0:T(8,128)S(1)}, f32[256,256]{1,0:T(8,128)}, u32[]{:S(2)}) copy-start(f32[256,256]{1,0:T(8,128)} %velocity_ref.1) | copy-start | bytes 786436
  8.2 25.2 %copy-start.1 = (f32[1,256,256]{2,1,0:T(8,128)S(1)}, f32[1,256,256]{2,1,0:T(8,128)}, u32[]{:S(2)}) copy-start(f32[1,256,256]{2,1,0:T(8,128)} %profile_ref.1) | copy-start | bytes 786436
  8.2 25.2 %copy-start.8 = (f32[128,256]{1,0:T(8,128)S(1)}, f32[128,256]{1,0:T(8,128)}, u32[]{:S(2)}) copy-start(f32[128,256]{1,0:T(8,128)} %constant.49.clone.columns_table) | copy-start | bytes 393220
  33.4 47.7 %copy-start.11 = (f32[128]{0:T(128)S(1)}, f32[128]{0:T(128)}, u32[]{:S(2)}) copy-start(f32[128]{0:T(128)} %constant.50.clone) | copy-start | bytes 1540
  33.4 60.9 %copy-start.2 = (f32[128,128]{1,0:T(8,128)S(1)}, f32[128,128]{1,0:T(8,128)}, u32[]{:S(2)}) copy-start(f32[128,128]{1,0:T(8,128)} %constant.51.clone.table_ref) | copy-start | bytes 196612
  33.4 60.9 %copy-start.9 = (f32[128,1]{1,0:T(8,128)S(1)}, f32[128,1]{1,0:T(8,128)}, u32[]{:S(2)}) copy-start(f32[128,1]{1,0:T(8,128)} %constant.52.clone.symbol_depth) | copy-start | bytes 1540
  33.5 60.8 %copy-start.10 = (f32[1,128]{1,0:T(1,128)S(1)}, f32[1,128]{1,0:T(1,128)}, u32[]{:S(2)}) copy-start(f32[1,128]{1,0:T(1,128)} %constant.53.clone.symbol_rows) | copy-start | bytes 1540
  69.7 24.6 %all-to-all-start = ((f32[128,8,128]{2,1,0:T(8,128)}), f32[128,8,128]{2,1,0:T(8,128)S(1)}, u32[]{:S(2)}, u32[]{:S(2)}) async-start(f32[128,8,128]{2,1,0:T(8,128)} %bitcast.8), calls=%async_computation | async-start | bytes 1048576 | tf_op jit(solution)/shard_map/all_to_all | solution.py:743
